TPU v7x, 32 devices: a whole 2x2x4 slice. The times are simulated.
32 devices in a mesh: dp: 2 (over x), expert: 16 (over z, y, core).
Axes of the slice: x: 2, y: 2, z: 4, core: 2. Of those that a mesh axis runs over, the one named last changes fastest.
Arguments:
- preactivations: bfloat16 [512, 8, 1536], P(('dp', 'expert')), may hold values from -6 to 6
- route_weights: float32 [512, 8], P(('dp', 'expert')), may hold values from 0.05 to 0.3
- expert_ids: int32 [512, 8], P(('dp', 'expert')), may hold values from 0 to 15, all different within a row; in each aligned block of 16 rows (0 to 15, 16 to 31, ...) at most 16 rows name the same one
- down_proj: bfloat16 [16, 4096, 768], P('expert'), may hold values from -0.21875 to 0.21875
- output_cotangent: bfloat16 [512, 4096], P(('dp', 'expert')), may hold values from -1.5 to 1.5
Outputs:
- mixed: bfloat16 [512, 4096], P(('dp', 'expert'))
- route_grads: float32 [512, 8], P(('dp', 'expert'))
- pre_grads: bfloat16 [512, 8, 1536], P(('dp', 'expert'))
- down_grads: float32 [16, 4096, 768], P('expert', 'dp')
Inputs may be any that keep to these rules, and one draw needn't show every extreme that they name: `expert_ids`: among the 128 slots of one device's tokens, no expert is named more than 16 times, a bound that some block reaches; a token's 8 experts are distinct.
All inputs are finite; a program needn't handle non-finite values.
Results may differ from a plain program's by a relative error of at most 0.017.
Values may be sent and summed in bfloat16 or wider, within the bound.
A program may use at most 64 MiB of HBM per device.

v0:
```python
import jax
import jax.numpy as jnp
from jax import lax
from jax.sharding import PartitionSpec as P


def slot_matrix(expert_ids, experts, capacity):
    slot_count = expert_ids.shape[0] * expert_ids.shape[1]
    flat_ids = expert_ids.reshape(slot_count)
    onehot = (flat_ids[:, None] == lax.iota(jnp.int32, experts)[None, :]).astype(jnp.float32)
    slot_order = lax.iota(jnp.int32, slot_count)
    earlier = (slot_order[:, None] > slot_order[None, :]).astype(jnp.float32)
    before = jnp.dot(earlier, onehot, preferred_element_type=jnp.float32)
    slot_rank = jnp.sum(before * onehot, axis=1).astype(jnp.int32)
    target = flat_ids * capacity + slot_rank
    return (lax.iota(jnp.int32, experts * capacity)[:, None] == target[None, :]).astype(
        jnp.bfloat16
    )


def on_device(preactivations, route_weights, expert_ids, down_proj, output_cotangent):
    token_count, per_token, pre_width = preactivations.shape
    hidden_units = pre_width // 2
    model_width = output_cotangent.shape[1]
    experts = lax.axis_size("expert")
    capacity = min(token_count, max(2, 2 * token_count * per_token // experts))
    slot_count = token_count * per_token
    row_count = experts * capacity
    placement = slot_matrix(expert_ids, experts, capacity)
    pre_vals = preactivations.reshape(slot_count, pre_width).astype(jnp.float32)
    gate_pre = pre_vals[:, :hidden_units]
    up_pre = pre_vals[:, hidden_units:]
    sigmoid_gate = jax.nn.sigmoid(gate_pre)
    activated = gate_pre * sigmoid_gate
    hidden = (activated * up_pre).astype(jnp.bfloat16)
    cotangent = output_cotangent.astype(jnp.float32)
    scaled = (
        (route_weights[:, :, None] * cotangent[:, None, :])
        .astype(jnp.bfloat16)
        .reshape(slot_count, model_width)
    )
    send_hidden = jnp.dot(placement, hidden, preferred_element_type=jnp.float32).astype(
        jnp.bfloat16
    )
    send_hidden = send_hidden.reshape(experts, capacity, hidden_units)
    send_cot = jnp.dot(placement, scaled, preferred_element_type=jnp.float32).astype(jnp.bfloat16)
    send_cot = send_cot.reshape(experts, capacity, model_width)
    weight = down_proj[0]
    recv_hidden = lax.all_to_all(send_hidden, "expert", split_axis=0, concat_axis=0, tiled=True)
    recv_cot = lax.all_to_all(send_cot, "expert", split_axis=0, concat_axis=0, tiled=True)
    expert_out = jnp.einsum(
        "scf,df->scd", recv_hidden, weight, preferred_element_type=jnp.float32
    ).astype(jnp.bfloat16)
    hidden_grad = jnp.einsum(
        "scd,df->scf", recv_cot, weight, preferred_element_type=jnp.float32
    ).astype(jnp.bfloat16)
    returned_out = lax.all_to_all(expert_out, "expert", split_axis=0, concat_axis=0, tiled=True)
    returned_grad = lax.all_to_all(hidden_grad, "expert", split_axis=0, concat_axis=0, tiled=True)
    returned_out, returned_grad, recv_hidden, recv_cot = (
        returned_out,
        returned_grad,
        recv_hidden,
        recv_cot,
    )
    slot_outs = jnp.dot(
        placement.T,
        returned_out.reshape(row_count, model_width),
        preferred_element_type=jnp.float32,
    )
    slot_grad = jnp.dot(
        placement.T,
        returned_grad.reshape(row_count, hidden_units),
        preferred_element_type=jnp.float32,
    )
    slot_outs = slot_outs.reshape(token_count, per_token, model_width)
    mixed = jnp.einsum("tk,tkd->td", route_weights, slot_outs).astype(jnp.bfloat16)
    route_grads = jnp.einsum("tkd,td->tk", slot_outs, cotangent)
    gate_grad = slot_grad * up_pre * (sigmoid_gate * (1.0 + gate_pre * (1.0 - sigmoid_gate)))
    up_grad = slot_grad * activated
    pre_grads = (
        jnp.concatenate([gate_grad, up_grad], axis=1)
        .astype(jnp.bfloat16)
        .reshape(token_count, per_token, pre_width)
    )
    hidden_rows = recv_hidden.reshape(row_count, hidden_units)
    cot_rows = recv_cot.reshape(row_count, model_width)
    weight_grads = lax.psum_scatter(
        lax.dot_general(
            cot_rows, hidden_rows, (((0,), (0,)), ((), ())), preferred_element_type=jnp.float32
        ).astype(jnp.bfloat16),
        "dp",
        scatter_dimension=0,
        tiled=True,
    ).astype(jnp.float32)
    return (mixed, route_grads, pre_grads, weight_grads[None])


def solution(mesh):
    in_specs = (
        P(("dp", "expert"), None, None),
        P(("dp", "expert"), None),
        P(("dp", "expert"), None),
        P("expert", None, None),
        P(("dp", "expert"), None),
    )
    out_specs = (
        P(("dp", "expert"), None),
        P(("dp", "expert"), None),
        P(("dp", "expert"), None, None),
        P("expert", "dp", None),
    )
    return jax.shard_map(
        on_device, mesh=mesh, in_specs=in_specs, out_specs=out_specs, check_vma=False
    )
```

profile of v0, /device:TPU:0, one launch (start us, length us, event | category | flops | bytes accessed | tf_op | source)
XLA Modules:
  0.0 176.1 jit_solution(5253375303643684939)
XLA Ops:
  7.2 0.0 copy-start.2
  7.2 0.0 copy-start.1
  7.2 0.8 copy.11
  8.0 0.1 reshape.75
  8.1 0.2 fusion.11
  8.2 1.1 bitcast_convert_fusion.2
  9.3 1.1 convolution_convert_fusion.1
  10.4 7.4 %all-to-all-start = ((bf16[16,16,768]{2,1,0:T(8,128)(2,1)}), bf16[16,16,768]{2,1,0:T(8,128)(2,1)S(1)}, u32[]{:S(2)}, u32[]{:S(2)}) async-start(bf16[16,16,768]{2,1,0:T(8,128)(2,1)} %bitcast.3), calls=%async_computation | async-start | bytes 786432 | tf_op jit(solution)/shard_map/all_to_all | solution.py:49
  17.8 0.0 reduce-scatter.2.cloned.1.call-start
  17.9 0.0 copy-done.2
  17.9 0.1 copy.12
  17.9 0.1 mul.57
  18.0 0.0 copy-done.1
  18.1 0.8 convolution_convert_fusion
  18.8 11.2 %all-to-all-done = bf16[16,16,768]{2,1,0:T(8,128)(2,1)S(1)} async-done(((bf16[16,16,768]{2,1,0:T(8,128)(2,1)}), bf16[16,16,768]{2,1,0:T(8,128)(2,1)S(1)}, u32[]{:S(2)}, u32[]{:S(2)}) %all-to-all-start) | async-done | bytes 393248 | tf_op jit(solution)/shard_map/all_to_all | solution.py:49
  30.0 50.6 %all_to_all.20 = bf16[16,16,4096]{2,1,0:T(8,128)(2,1)S(1)} all-to-all(bf16[16,16,4096]{2,1,0:T(8,128)(2,1)S(1)} %bitcast.52), channel_id=1, replica_groups=mesh['dp'=2,'expert'=16] {'expert'}, dimensions={0} | all-to-all | bytes 4194304 | tf_op jit(solution)/shard_map/all_to_all | solution.py:50
  80.6 0.0 copy-start
  80.6 1.3 copy-done
  82.0 4.6 %bitcast_convert_fusion = bf16[4096,768]{1,0:T(8,128)(2,1)} fusion(bf16[16,16,4096]{2,1,0:T(8,128)(2,1)S(1)} %all_to_all.20, bf16[16,16,768]{2,1,0:T(8,128)(2,1)S(1)} %all-to-all-done), kind=kOutput, calls=%fused_computation | convolution fusion | flops 1613758464 | bytes 8781824 | tf_op jit(solution)/shard_map/dot_general | solution.py:88
  86.6 0.0 reduce-scatter.2.cloned.1.call-update
  86.6 6.0 %fusion.4 = bf16[16,16,4096]{2,1,0:T(8,128)(2,1)} fusion(bf16[16,16,768]{2,1,0:T(8,128)(2,1)S(1)} %all-to-all-done, bf16[1,4096,768]{2,1,0:T(8,128)(2,1)} %param.8), kind=kOutput, calls=%fused_computation.6 | convolution fusion | flops 1611661312 | bytes 8781824 | tf_op jit(solution)/shard_map/scf,df->scd/dot_general | solution.py:51
  92.6 5.1 %all-to-all-start.1 = ((bf16[16,16,4096]{2,1,0:T(8,128)(2,1)}), bf16[16,16,4096]{2,1,0:T(8,128)(2,1)S(1)}, u32[]{:S(2)}, u32[]{:S(2)}) async-start(bf16[16,16,4096]{2,1,0:T(8,128)(2,1)} %fusion.4), calls=%async_computation.1 | async-start | bytes 4194304 | tf_op jit(solution)/shard_map/all_to_all | solution.py:57
  97.7 0.1 copy.13
  97.7 6.0 %fusion.8 = bf16[16,16,768]{2,1,0:T(8,128)(2,1)} fusion(bf16[16,16,4096]{2,1,0:T(8,128)(2,1)} %copy-done, bf16[1,4096,768]{2,1,0:T(8,128)(2,1)} %param.8), kind=kOutput, calls=%fused_computation.11 | convolution fusion | flops 1610809344 | bytes 8781824 | tf_op jit(solution)/shard_map/scd,df->scf/dot_general | solution.py:54
  103.7 35.1 %all-to-all-done.1 = bf16[16,16,4096]{2,1,0:T(8,128)(2,1)S(1)} async-done(((bf16[16,16,4096]{2,1,0:T(8,128)(2,1)}), bf16[16,16,4096]{2,1,0:T(8,128)(2,1)S(1)}, u32[]{:S(2)}, u32[]{:S(2)}) %all-to-all-start.1) | async-done | bytes 2097184 | tf_op jit(solution)/shard_map/all_to_all | solution.py:57
  138.8 11.2 %all-to-all-start.3 = ((bf16[16,16,768]{2,1,0:T(8,128)(2,1)}), bf16[16,16,768]{2,1,0:T(8,128)(2,1)S(1)}, u32[]{:S(2)}, u32[]{:S(2)}) async-start(bf16[16,16,768]{2,1,0:T(8,128)(2,1)} %fusion.8), calls=%async_computation.3 | async-start | bytes 786432 | tf_op jit(solution)/shard_map/all_to_all | solution.py:58
  150.0 0.5 fusion.22
  150.5 0.4 fusion.31
  150.9 0.8 copy.20
  151.7 0.8 fusion.16
  152.5 0.7 copy.16
  153.2 9.0 %all-to-all-done.3 = bf16[16,16,768]{2,1,0:T(8,128)(2,1)S(1)} async-done(((bf16[16,16,768]{2,1,0:T(8,128)(2,1)}), bf16[16,16,768]{2,1,0:T(8,128)(2,1)S(1)}, u32[]{:S(2)}, u32[]{:S(2)}) %all-to-all-start.3) | async-done | bytes 393248 | tf_op jit(solution)/shard_map/all_to_all | solution.py:58
  162.2 0.3 fusion.19
  162.5 0.8 pad_maximum_fusion
  163.3 0.9 reduce-scatter.2.cloned.1.call-done
  164.2 5.1 %bitcast_convert_fusion.1 = f32[1,2048,768]{2,1,0:T(8,128)} fusion(bf16[2048,768]{1,0:T(8,128)(2,1)} %reduce-scatter.2.cloned.1.call-done), kind=kLoop, calls=%fused_computation.7 | loop fusion | flops 1572864 | bytes 9437184 | tf_op jit(solution)/shard_map/broadcast_in_dim | solution.py:95
  (2 shorter events, 0.0 us)
Async XLA Ops:
  7.2 10.7 %copy-start.2 = (f32[16,8]{0,1:T(8,128)S(1)}, f32[16,8]{0,1:T(8,128)}, u32[]{:S(2)}) copy-start(f32[16,8]{0,1:T(8,128)} %param.6) | copy-start | bytes 1540
  7.2 10.8 %copy-start.1 = (bf16[16,4096]{1,0:T(8,128)(2,1)S(1)}, bf16[16,4096]{1,0:T(8,128)(2,1)}, u32[]{:S(2)}) copy-start(bf16[16,4096]{1,0:T(8,128)(2,1)} %param.9) | copy-start | bytes 393220
  10.4 19.6 %all-to-all-start = ((bf16[16,16,768]{2,1,0:T(8,128)(2,1)}), bf16[16,16,768]{2,1,0:T(8,128)(2,1)S(1)}, u32[]{:S(2)}, u32[]{:S(2)}) async-start(bf16[16,16,768]{2,1,0:T(8,128)(2,1)} %bitcast.3), calls=%async_computation | async-start | bytes 786432 | tf_op jit(solution)/shard_map/all_to_all | solution.py:49
  17.8 146.4 %reduce-scatter.2.cloned.1.call-start = ((), (), s32[]{:S(2)}) async-start(), calls=%async_computation.5 | async-start | bytes 9437184 | tf_op jit(solution)/shard_map/reduce_scatter | solution.py:87
  80.6 1.4 copy-start
  92.6 46.2 %all-to-all-start.1 = ((bf16[16,16,4096]{2,1,0:T(8,128)(2,1)}), bf16[16,16,4096]{2,1,0:T(8,128)(2,1)S(1)}, u32[]{:S(2)}, u32[]{:S(2)}) async-start(bf16[16,16,4096]{2,1,0:T(8,128)(2,1)} %fusion.4), calls=%async_computation.1 | async-start | bytes 4194304 | tf_op jit(solution)/shard_map/all_to_all | solution.py:57
  138.8 23.4 %all-to-all-start.3 = ((bf16[16,16,768]{2,1,0:T(8,128)(2,1)}), bf16[16,16,768]{2,1,0:T(8,128)(2,1)S(1)}, u32[]{:S(2)}, u32[]{:S(2)}) async-start(bf16[16,16,768]{2,1,0:T(8,128)(2,1)} %fusion.8), calls=%async_computation.3 | async-start | bytes 786432 | tf_op jit(solution)/shard_map/all_to_all | solution.py:58
Sparse Core Ops, SparseCore 0:
  86.7 77.4 reduce-scatter.1
where the time goes:
time: 177 us; the launch traced here: 176 us
  waiting for transfers between devices  56.2 us (32%)
  blocking collectives  50.6 us (29%)
  starting transfers between devices  23.7 us (13%)
  matrix products  20.5 us (12%)
  between operations  14.1 us (8%)
  other arithmetic  6.96 us (4%)
  local copies, waits for them, and re-layouts  3.96 us (2%)
    all_to_all x1, blocking collectives, on_device(): lax.all_to_all(send_cot, 'expert', split_axis=0, concat_axis=0, tiled=True)  50.6 us
    all_to_all x1, waiting for transfers between devices, on_device(): lax.all_to_all(expert_out, 'expert', split_axis=0, concat_axis=0, tiled=T...  35.1 us
    all_to_all x1, starting transfers between devices, on_device(): lax.all_to_all(hidden_grad, 'expert', split_axis=0, concat_axis=0, tiled=...  11.2 us
    all_to_all x1, waiting for transfers between devices, on_device(): lax.all_to_all(send_hidden, 'expert', split_axis=0, concat_axis=0, tiled=...  11.2 us
    all_to_all x1, waiting for transfers between devices, on_device(): lax.all_to_all(hidden_grad, 'expert', split_axis=0, concat_axis=0, tiled=...  9.02 us
    all_to_all x1, starting transfers between devices, on_device(): lax.all_to_all(send_hidden, 'expert', split_axis=0, concat_axis=0, tiled=...  7.39 us
    dot_general x1, matrix products, on_device(): jnp.einsum('scf,df->scd', recv_hidden, weight, preferred_element_type=jnp...  5.97 us
    dot_general x1, matrix products, on_device(): jnp.einsum('scd,df->scf', recv_cot, weight, preferred_element_type=jnp.fl...  5.96 us
  transfers between devices with their start and end apart: 4, of which 4 were waited for; matrix products, arithmetic and copies ran while one was open for 10% of the time, Pallas kernels for 0%

commit v1 on v0

v1 whole, which is shorter than its diff:
```python
import jax
import jax.numpy as jnp
from jax import lax
from jax.sharding import PartitionSpec as P


def on_device(preactivations, route_weights, expert_ids, down_proj, output_cotangent):
    token_count, per_token, pre_width = preactivations.shape
    hidden_units = pre_width // 2
    model_width = output_cotangent.shape[1]
    experts = lax.axis_size("expert")
    copies = lax.axis_size("dp")
    slot_count = token_count * per_token
    flat_ids = expert_ids.reshape(slot_count)
    slot_token = lax.iota(jnp.int32, slot_count) // per_token
    target = flat_ids * token_count + slot_token
    placement = (
        lax.iota(jnp.int32, experts * token_count)[:, None] == target[None, :]
    ).astype(jnp.bfloat16)
    pre_vals = preactivations.reshape(slot_count, pre_width).astype(jnp.float32)
    gate_pre = pre_vals[:, :hidden_units]
    up_pre = pre_vals[:, hidden_units:]
    sigmoid_gate = jax.nn.sigmoid(gate_pre)
    activated = gate_pre * sigmoid_gate
    hidden = activated * up_pre
    slot_weight = route_weights.reshape(slot_count, 1)
    weighted = (slot_weight * hidden).astype(jnp.bfloat16)
    weight = down_proj[0]

    cot_rows = lax.all_gather(output_cotangent, "expert", axis=0, tiled=True)
    send = jnp.dot(placement, weighted, preferred_element_type=jnp.float32).astype(jnp.bfloat16)
    send = send.reshape(experts, token_count, hidden_units)
    recv = lax.all_to_all(send, "expert", split_axis=0, concat_axis=0, tiled=True)
    hidden_rows = recv.reshape(experts * token_count, hidden_units)

    mixed_part = lax.dot_general(
        hidden_rows, weight, (((1,), (1,)), ((), ())), preferred_element_type=jnp.float32
    ).astype(jnp.bfloat16)
    mixed = lax.psum_scatter(mixed_part, "expert", scatter_dimension=0, tiled=True)

    grad_rows = jnp.dot(cot_rows, weight, preferred_element_type=jnp.float32).astype(jnp.bfloat16)
    grad_back = lax.all_to_all(
        grad_rows.reshape(experts, token_count, hidden_units),
        "expert",
        split_axis=0,
        concat_axis=0,
        tiled=True,
    ).reshape(experts * token_count, hidden_units)

    if copies == 2:
        half = model_width // 2
        mine = lax.axis_index("dp")
        swap = [(0, 1), (1, 0)]
        cot_keep = lax.dynamic_slice_in_dim(cot_rows, mine * half, half, 1)
        cot_give = lax.dynamic_slice_in_dim(cot_rows, (1 - mine) * half, half, 1)
        cot_other = lax.ppermute(cot_give, "dp", swap)
        hidden_other = lax.ppermute(hidden_rows, "dp", swap)
        contract = (((0,), (0,)), ((), ()))
        weight_grads = lax.dot_general(
            cot_keep, hidden_rows, contract, preferred_element_type=jnp.float32
        ) + lax.dot_general(
            cot_other, hidden_other, contract, preferred_element_type=jnp.float32
        )
    else:
        weight_grads = lax.psum_scatter(
            lax.dot_general(
                cot_rows, hidden_rows, (((0,), (0,)), ((), ())), preferred_element_type=jnp.float32
            ).astype(jnp.bfloat16),
            "dp",
            scatter_dimension=0,
            tiled=True,
        ).astype(jnp.float32)

    slot_grad = lax.dot_general(
        placement, grad_back, (((0,), (0,)), ((), ())), preferred_element_type=jnp.float32
    )
    route_grads = jnp.sum(slot_grad * hidden, axis=1).reshape(token_count, per_token)
    hidden_grad = slot_weight * slot_grad
    gate_grad = hidden_grad * up_pre * (sigmoid_gate * (1.0 + gate_pre * (1.0 - sigmoid_gate)))
    up_grad = hidden_grad * activated
    pre_grads = (
        jnp.concatenate([gate_grad, up_grad], axis=1)
        .astype(jnp.bfloat16)
        .reshape(token_count, per_token, pre_width)
    )
    return (mixed, route_grads, pre_grads, weight_grads[None])


def solution(mesh):
    in_specs = (
        P(("dp", "expert"), None, None),
        P(("dp", "expert"), None),
        P(("dp", "expert"), None),
        P("expert", None, None),
        P(("dp", "expert"), None),
    )
    out_specs = (
        P(("dp", "expert"), None),
        P(("dp", "expert"), None),
        P(("dp", "expert"), None, None),
        P("expert", "dp", None),
    )
    return jax.shard_map(
        on_device, mesh=mesh, in_specs=in_specs, out_specs=out_specs, check_vma=False
    )
```

time: 177 us -> 128 us (0.72)
  blocking collectives: 50.6 us -> 22.4 us
  starting transfers between devices: 23.7 us -> 6.37 us
  matrix products: 20.5 us -> 25 us
  other arithmetic: 6.96 us -> 2.54 us
    all_to_all x3 -> x1, waiting for transfers between devices: 55.3 us -> 6.24 us  [on_device(): lax.all_to_all(grad_rows.reshape(experts, token_count, hidden_units), 'ex...]
    all_to_all x1, blocking collectives: 50.6 us -> 22.4 us  [on_device(): lax.all_to_all(send, 'expert', split_axis=0, concat_axis=0, tiled=True)]
    all_to_all x3 -> x1, starting transfers between devices: 23.7 us -> 4.21 us  [on_device(): lax.all_to_all(grad_rows.reshape(experts, token_count, hidden_units), 'ex...]
    ppermute x0 -> x2, waiting for transfers between devices: none -> 18.6 us  [the longest x1 18.6 us: on_device(): hidden_other = lax.ppermute(hidden_rows, 'dp', swap)]
    all_gather x0 -> x1, waiting for transfers between devices: none -> 16.4 us  [on_device(): cot_rows = lax.all_gather(output_cotangent, 'expert', axis=0, tiled=True)]
    reduce_scatter x1, waiting for transfers between devices: 0.92 us -> 13.3 us  [on_device(): lax.psum_scatter(mixed_part, 'expert', scatter_dimension=0, tiled=True)]
    broadcast_in_dim x1 -> x0, other arithmetic: 5.08 us -> none  [on_device(): return (mixed, route_grads, pre_grads, weight_grads[None])]
    dot_general x10 -> x6, matrix products: 20.5 us -> 25 us  [the longest x1 7.06 us: on_device(): lax.dot_general(cot_other, hidden_other, contract, preferred_element_type...]
  transfers between devices with their start and end apart: 4 -> 5, of which waited for: 4 -> 4; matrix products, arithmetic and copies ran while one was open for 10% -> 23% of each run, Pallas kernels for 0% -> 0%
where the time goes in v1:
time: 128 us
  waiting for transfers between devices  55.2 us (43%)
  matrix products  25 us (20%)
  blocking collectives  22.4 us (18%)
  between operations  14.1 us (11%)
  starting transfers between devices  6.37 us (5%)
  other arithmetic  2.54 us (2%)
  local copies, waits for them, and re-layouts  2.4 us (2%)
    all_to_all x1, blocking collectives, on_device(): lax.all_to_all(send, 'expert', split_axis=0, concat_axis=0, tiled=True)  22.4 us
    ppermute x1, waiting for transfers between devices, on_device(): hidden_other = lax.ppermute(hidden_rows, 'dp', swap)  18.6 us
    all_gather x1, waiting for transfers between devices, on_device(): cot_rows = lax.all_gather(output_cotangent, 'expert', axis=0, tiled=True)  16.4 us
    reduce_scatter x1, waiting for transfers between devices, on_device(): lax.psum_scatter(mixed_part, 'expert', scatter_dimension=0, tiled=True)  13.3 us
    dot_general x1, matrix products, on_device(): lax.dot_general(cot_other, hidden_other, contract, preferred_element_type...  7.06 us
    all_to_all x1, waiting for transfers between devices, on_device(): lax.all_to_all(grad_rows.reshape(experts, token_count, hidden_units), 'ex...  6.24 us
    dot_general x1, matrix products, on_device(): jnp.dot(cot_rows, weight, preferred_element_type=jnp.float32)  6.09 us
    dot_general x1, matrix products, on_device(): lax.dot_general(hidden_rows, weight, (((1,), (1,)), ((), ())), preferred_...  6.02 us
  transfers between devices with their start and end apart: 5, of which 4 were waited for; matrix products, arithmetic and copies ran while one was open for 23% of the time, Pallas kernels for 0%

profile of v1, /device:TPU:0, one launch (start us, length us, event | category | flops | bytes accessed | tf_op | source)
XLA Modules:
  0.0 128.0 jit_solution(15187856835957708215)
XLA Ops:
  7.2 0.0 all-gather.2.cloned.1.call-start
  7.2 0.7 all-gather.2.cloned.1.call-update
  7.9 0.0 reduce-scatter.2.cloned.1.call-start
  7.9 0.8 copy.13
  8.7 0.1 mul.62
  8.8 0.7 broadcast_multiply_fusion
  9.5 0.1 copy.12
  9.6 0.1 mul.61
  9.7 1.1 bitcast_convert_fusion
  10.7 0.0 copy-start.1
  10.7 0.4 convolution_convert_fusion
  11.1 0.5 copy-done.1
  11.6 22.4 %all_to_all.10 = bf16[16,16,768]{2,1,0:T(8,128)(2,1)S(1)} all-to-all(bf16[16,16,768]{2,1,0:T(8,128)(2,1)S(1)} %bitcast.31), channel_id=1, replica_groups=mesh['dp'=2,'expert'=16] {'expert'}, dimensions={0} | all-to-all | bytes 786432 | tf_op jit(solution)/shard_map/all_to_all | solution.py:33
  34.0 6.0 %fusion.4 = bf16[256,4096]{1,0:T(8,128)(2,1)} fusion(bf16[256,768]{1,0:T(8,128)(2,1)S(1)} %bitcast.28, bf16[1,4096,768]{2,1,0:T(8,128)(2,1)} %param.8), kind=kOutput, calls=%fused_computation.5 | convolution fusion | flops 1611661312 | bytes 8781824 | tf_op jit(solution)/shard_map/dot_general | solution.py:36
  40.0 0.0 reduce-scatter.2.cloned.1.call-update
  40.1 16.4 %all-gather.2.cloned.1.call-done = bf16[256,4096]{1,0:T(8,128)(2,1)} async-done(((bf16[16,4096]{1,0:T(8,128)(2,1)}), bf16[256,4096]{1,0:T(8,128)(2,1)}) %all-gather.2.cloned.1.call-update) | async-done | bytes 2097168 | tf_op jit(solution)/shard_map/all_gather | solution.py:30
  56.5 0.0 copy-start
  56.5 6.1 %fusion.7 = bf16[256,768]{1,0:T(8,128)(2,1)} fusion(bf16[256,4096]{1,0:T(8,128)(2,1)} %all-gather.2.cloned.1.call-done, bf16[1,4096,768]{2,1,0:T(8,128)(2,1)} %param.8), kind=kOutput, calls=%fused_computation.7 | convolution fusion | flops 1610809344 | bytes 8781824 | tf_op jit(solution)/shard_map/dot_general | solution.py:41
  62.6 4.2 %all-to-all-start.1 = ((bf16[16,16,768]{2,1,0:T(8,128)(2,1)}), bf16[16,16,768]{2,1,0:T(8,128)(2,1)}, u32[]{:S(2)}, u32[]{:S(2)}) async-start(bf16[16,16,768]{2,1,0:T(8,128)(2,1)} %bitcast.5), calls=%async_computation.2 | async-start | bytes 786432 | tf_op jit(solution)/shard_map/all_to_all | solution.py:42
  66.8 0.0 copy-done
  66.8 0.1 constant_dynamic-slice_fusion
  66.9 1.5 %collective-permute-start = (bf16[256,2048]{1,0:T(8,128)(2,1)S(1)}, bf16[256,2048]{1,0:T(8,128)(2,1)}, u32[]{:S(2)}, u32[]{:S(2)}) collective-permute-start(bf16[256,2048]{1,0:T(8,128)(2,1)S(1)} %constant_dynamic-slice_fusion), channel_id=1, source_target_pairs={{0,16},{16,0},{1,17},{17,1},{2,18},{18,2},{3,19},{19,3},{4,20},{20... | collective-permute-start | bytes 3145736 | tf_op jit(solution)/shard_map/ppermute | solution.py:56
  68.5 0.6 collective-permute-start.1
  69.0 3.7 %fusion.10 = f32[2048,768]{1,0:T(8,128)} fusion(bf16[256,768]{1,0:T(8,128)(2,1)S(1)} %bitcast.30, bf16[256,4096]{1,0:T(8,128)(2,1)S(1)} %copy-done, s32[]{:T(128)S(6)} %select_n.16), kind=kOutput, calls=%fused_computation.8 | convolution fusion | flops 805306368 | bytes 7733252 | tf_op jit(solution)/shard_map/dot_general | solution.py:59
  72.8 6.2 %all-to-all-done.1 = bf16[16,16,768]{2,1,0:T(8,128)(2,1)} async-done(((bf16[16,16,768]{2,1,0:T(8,128)(2,1)}), bf16[16,16,768]{2,1,0:T(8,128)(2,1)}, u32[]{:S(2)}, u32[]{:S(2)}) %all-to-all-start.1) | async-done | bytes 393248 | tf_op jit(solution)/shard_map/all_to_all | solution.py:42
  79.0 1.7 %fusion.15 = (bf16[16,8,768]{2,1,0:T(8,128)(2,1)S(1)}, bf16[16,8,768]{2,1,0:T(8,128)(2,1)S(1)}, f32[128]{0:T(128)S(1)}) fusion(f32[128,1536]{1,0:T(8,128)} %copy-done.1, f32[128]{0:T(128)S(1)} %mul.62, bf16[256,768]{1,0:T(8,128)(2,1)} %bitcast.6, s32[128]{0:T(128)S(1)} %fusion.19), kind=kOutput, calls=%fused_computation.21 | convolution fusion | flops 52035456 | bytes 1574400 | tf_op jit(solution)/shard_map/dot_general | solution.py:74
  80.7 0.1 reshape.59
  80.8 0.7 copy.14
  81.5 0.8 pad_maximum_fusion
  82.2 18.6 %collective-permute-done.1 = bf16[256,768]{1,0:T(8,128)(2,1)} collective-permute-done((bf16[256,768]{1,0:T(8,128)(2,1)S(1)}, bf16[256,768]{1,0:T(8,128)(2,1)}, u32[]{:S(2)}, u32[]{:S(2)}) %collective-permute-start.1) | collective-permute-done | bytes 393248 | tf_op jit(solution)/shard_map/ppermute | solution.py:57
  100.8 0.0 collective-permute-done
  100.8 7.1 %add_bitcast_fusion = f32[1,2048,768]{2,1,0:T(8,128)} fusion(f32[2048,768]{1,0:T(8,128)} %fusion.10, bf16[256,2048]{1,0:T(8,128)(2,1)} %collective-permute-done, bf16[256,768]{1,0:T(8,128)(2,1)} %collective-permute-done.1), kind=kOutput, calls=%fused_computation.4 | convolution fusion | flops 806879232 | bytes 14024704 | tf_op jit(solution)/shard_map/dot_general | solution.py:61
  107.9 13.3 %reduce-scatter.2.cloned.1.call-done = bf16[16,4096]{1,0:T(8,128)(2,1)} async-done(((bf16[256,4096]{1,0:T(8,128)(2,1)}), bf16[16,4096]{1,0:T(8,128)(2,1)}) %reduce-scatter.2.cloned.1.call-update) | async-done | bytes 131088 | tf_op jit(solution)/shard_map/reduce_scatter | solution.py:39
  (1 shorter events, 0.0 us)
Async XLA Ops:
  7.2 49.3 %all-gather.2.cloned.1.call-start = ((), (), s32[]{:S(2)}) async-start(), calls=%async_computation.4 | async-start | bytes 2228224 | tf_op jit(solution)/shard_map/all_gather | solution.py:30
  7.9 113.2 %reduce-scatter.2.cloned.1.call-start = ((), (), s32[]{:S(2)}) async-start(), calls=%async_computation.3 | async-start | bytes 2228224 | tf_op jit(solution)/shard_map/reduce_scatter | solution.py:39
  10.7 0.9 copy-start.1
  56.5 10.3 %copy-start = (bf16[256,4096]{1,0:T(8,128)(2,1)S(1)}, bf16[256,4096]{1,0:T(8,128)(2,1)}, u32[]{:S(2)}) copy-start(bf16[256,4096]{1,0:T(8,128)(2,1)} %all-gather.2.cloned.1.call-done) | copy-start | bytes 6291460
  62.6 16.4 %all-to-all-start.1 = ((bf16[16,16,768]{2,1,0:T(8,128)(2,1)}), bf16[16,16,768]{2,1,0:T(8,128)(2,1)}, u32[]{:S(2)}, u32[]{:S(2)}) async-start(bf16[16,16,768]{2,1,0:T(8,128)(2,1)} %bitcast.5), calls=%async_computation.2 | async-start | bytes 786432 | tf_op jit(solution)/shard_map/all_to_all | solution.py:42
  66.9 33.9 %collective-permute-start = (bf16[256,2048]{1,0:T(8,128)(2,1)S(1)}, bf16[256,2048]{1,0:T(8,128)(2,1)}, u32[]{:S(2)}, u32[]{:S(2)}) collective-permute-start(bf16[256,2048]{1,0:T(8,128)(2,1)S(1)} %constant_dynamic-slice_fusion), channel_id=1, source_target_pairs={{0,16},{16,0},{1,17},{17,1},{2,18},{18,2},{3,19},{19,3},{4,20},{20... | collective-permute-start | bytes 3145736 | tf_op jit(solution)/shard_map/ppermute | solution.py:56
  68.5 32.4 %collective-permute-start.1 = (bf16[256,768]{1,0:T(8,128)(2,1)S(1)}, bf16[256,768]{1,0:T(8,128)(2,1)}, u32[]{:S(2)}, u32[]{:S(2)}) collective-permute-start(bf16[256,768]{1,0:T(8,128)(2,1)S(1)} %bitcast.29), channel_id=1, source_target_pairs={{0,16},{16,0},{1,17},{17,1},{2,18},{18,2},{3,19},{19,3},{4,20},{20... | collective-permute-start | bytes 1179656 | tf_op jit(solution)/shard_map/ppermute | solution.py:57
Sparse Core Ops, SparseCore 0:
  10.2 46.2 all-gather.1
  60.8 60.2 reduce-scatter.1

commit v2 on v1

--- a/solution.py
+++ b/solution.py
@@ -1,7 +1,243 @@
+import functools
+
 import jax
 import jax.numpy as jnp
 from jax import lax
+from jax.experimental import pallas as pl
+from jax.experimental.pallas import tpu as pltpu
 from jax.sharding import PartitionSpec as P
+
+MESH = pl.DeviceIdType.MESH
+CHUNKS = 4
+
+
+def place(n):
+    me = lax.axis_index("expert")
+    return me, me // 4, (me // 2) % 2, me % 2, n // 4
+
+
+def greet(n):
+    me = lax.axis_index("expert")
+    barrier = pltpu.get_barrier_semaphore()
+    for step in range(1, n):
+        pl.semaphore_signal(
+            barrier, inc=1, device_id={"expert": (me + step) % n}, device_id_type=MESH
+        )
+    pl.semaphore_wait(barrier, n - 1)
+
+
+def spread_kernel(n, cot_ref, send_ref, cot_all, recv_all, own_sem, *sems):
+    far_s, far_r, near_s, near_r, core_s, core_r, swap_s, swap_r = sems
+    me, far, near, core, fars = place(n)
+
+    def remote(src, dst, send_sem, recv_sem, target):
+        copy = pltpu.make_async_remote_copy(
+            src_ref=src,
+            dst_ref=dst,
+            send_sem=send_sem,
+            recv_sem=recv_sem,
+            device_id={"expert": target},
+            device_id_type=MESH,
+        )
+        copy.start()
+        return copy
+
+    keep_cot = pltpu.make_async_copy(cot_ref, cot_all.at[me], own_sem.at[0])
+    keep_row = pltpu.make_async_copy(send_ref.at[me], recv_all.at[me], own_sem.at[1])
+    keep_cot.start()
+    keep_row.start()
+    greet(n)
+    sibling = me + 1 - 2 * core
+    beside = me + 2 - 4 * near
+
+    far_copies = [
+        remote(
+            cot_ref,
+            cot_all.at[me],
+            far_s.at[step - 1],
+            far_r.at[step - 1],
+            ((far + step) % fars) * 4 + near * 2 + core,
+        )
+        for step in range(1, fars)
+    ]
+    near_copies = [remote(cot_ref, cot_all.at[me], near_s.at[0], near_r.at[0], beside)]
+    core_copies = [remote(cot_ref, cot_all.at[me], core_s.at[0], core_r.at[0], sibling)]
+    swap_copies = []
+    for step in range(1, n):
+        target = (me + step) % n
+        swap_copies.append(
+            remote(
+                send_ref.at[target],
+                recv_all.at[me],
+                swap_s.at[step - 1],
+                swap_r.at[step - 1],
+                target,
+            )
+        )
+    for step in range(1, fars):
+        far_copies[step - 1].wait_recv()
+        block = ((far - step + fars) % fars) * 4 + near * 2 + core
+        ref = cot_all.at[block]
+        near_copies.append(remote(ref, ref, near_s.at[step], near_r.at[step], beside))
+        core_copies.append(remote(ref, ref, core_s.at[step], core_r.at[step], sibling))
+    for step in range(fars):
+        near_copies[step].wait_recv()
+        block = ((far - step + fars) % fars) * 4 + (1 - near) * 2 + core
+        ref = cot_all.at[block]
+        at = fars + step
+        core_copies.append(remote(ref, ref, core_s.at[at], core_r.at[at], sibling))
+    for copy in swap_copies + core_copies:
+        copy.wait_recv()
+    for copy in far_copies + near_copies + core_copies + swap_copies:
+        copy.wait_send()
+    keep_cot.wait()
+    keep_row.wait()
+
+
+def spread(cot, send):
+    n = lax.axis_size("expert")
+    tokens, width = cot.shape
+    hidden_units = send.shape[2]
+    dma = pltpu.SemaphoreType.DMA
+    return pl.pallas_call(
+        functools.partial(spread_kernel, n),
+        out_shape=(
+            jax.ShapeDtypeStruct((n, tokens, width), cot.dtype),
+            jax.ShapeDtypeStruct((n, tokens, hidden_units), send.dtype),
+        ),
+        in_specs=[pl.BlockSpec(memory_space=pltpu.VMEM)] * 2,
+        out_specs=[pl.BlockSpec(memory_space=pltpu.VMEM)] * 2,
+        scratch_shapes=[dma((2,))]
+        + [dma((n // 4 - 1,))] * 2
+        + [dma((n // 4,))] * 2
+        + [dma((n // 2,))] * 2
+        + [dma((n - 1,))] * 2,
+        compiler_params=pltpu.CompilerParams(
+            collective_id=0, has_side_effects=True, vmem_limit_bytes=32 * 1024 * 1024
+        ),
+    )(cot, send)
+
+
+def collect_kernel(n, part_ref, grad_ref, mixed_ref, back_ref, *scratch):
+    core_buf, core_sum, near_buf, near_sum, far_buf, own_sem = scratch[:6]
+    far_s, far_r, near_s, near_r, core_s, core_r, swap_s, swap_r = scratch[6:]
+    me, far, near, core, fars = place(n)
+    chunk = core_buf.shape[-1]
+
+    def remote(src, dst, send_sem, recv_sem, target):
+        copy = pltpu.make_async_remote_copy(
+            src_ref=src,
+            dst_ref=dst,
+            send_sem=send_sem,
+            recv_sem=recv_sem,
+            device_id={"expert": target},
+            device_id_type=MESH,
+        )
+        copy.start()
+        return copy
+
+    def added(left, right):
+        return (left.astype(jnp.float32) + right.astype(jnp.float32)).astype(jnp.bfloat16)
+
+    keep_row = pltpu.make_async_copy(grad_ref.at[me], back_ref.at[me], own_sem.at[0])
+    keep_row.start()
+    greet(n)
+    sibling = me + 1 - 2 * core
+    beside = me + 2 - 4 * near
+    core_copies = [
+        remote(
+            part_ref.at[1 - core, :, :, :, pl.ds(at * chunk, chunk)],
+            core_buf.at[at],
+            core_s.at[at],
+            core_r.at[at],
+            sibling,
+        )
+        for at in range(CHUNKS)
+    ]
+    near_copies, far_copies, swap_copies = [], [], []
+    for at in range(CHUNKS):
+        core_copies[at].wait_recv()
+        mine = part_ref[core, :, :, :, at * chunk : (at + 1) * chunk]
+        core_sum[at] = added(mine, core_buf[at])
+        near_copies.append(
+            remote(
+                core_sum.at[at, 1 - near],
+                near_buf.at[at],
+                near_s.at[at],
+                near_r.at[at],
+                beside,
+            )
+        )
+    for step in range(1, n):
+        target = (me + step) % n
+        swap_copies.append(
+            remote(
+                grad_ref.at[target],
+                back_ref.at[me],
+                swap_s.at[step - 1],
+                swap_r.at[step - 1],
+                target,
+            )
+        )
+    for at in range(CHUNKS):
+        near_copies[at].wait_recv()
+        near_sum[at] = added(core_sum[at, near], near_buf[at])
+        for step in range(1, fars):
+            target = (far + step) % fars
+            slot = at * (fars - 1) + step - 1
+            far_copies.append(
+                remote(
+                    near_sum.at[at, target],
+                    far_buf.at[at, step - 1],
+                    far_s.at[slot],
+                    far_r.at[slot],
+                    target * 4 + near * 2 + core,
+                )
+            )
+    for at in range(CHUNKS):
+        for step in range(1, fars):
+            far_copies[at * (fars - 1) + step - 1].wait_recv()
+        total = near_sum[at, far].astype(jnp.float32)
+        for step in range(1, fars):
+            total = total + far_buf[at, step - 1].astype(jnp.float32)
+        mixed_ref[:, at * chunk : (at + 1) * chunk] = total.astype(jnp.bfloat16)
+    for copy in swap_copies:
+        copy.wait_recv()
+    for copy in core_copies + near_copies + far_copies + swap_copies:
+        copy.wait_send()
+    keep_row.wait()
+
+
+def collect(part, grad):
+    n, tokens, hidden_units = grad.shape
+    width = part.shape[-1]
+    chunk = width // CHUNKS
+    fars = n // 4
+    dma = pltpu.SemaphoreType.DMA
+    far_count = CHUNKS * (fars - 1)
+    return pl.pallas_call(
+        functools.partial(collect_kernel, n),
+        out_shape=(
+            jax.ShapeDtypeStruct((tokens, width), part.dtype),
+            jax.ShapeDtypeStruct((n, tokens, hidden_units), grad.dtype),
+        ),
+        in_specs=[pl.BlockSpec(memory_space=pltpu.VMEM)] * 2,
+        out_specs=[pl.BlockSpec(memory_space=pltpu.VMEM)] * 2,
+        scratch_shapes=[
+            pltpu.VMEM((CHUNKS, 2, fars, tokens, chunk), part.dtype),
+            pltpu.VMEM((CHUNKS, 2, fars, tokens, chunk), part.dtype),
+            pltpu.VMEM((CHUNKS, fars, tokens, chunk), part.dtype),
+            pltpu.VMEM((CHUNKS, fars, tokens, chunk), part.dtype),
+            pltpu.VMEM((CHUNKS, fars - 1, tokens, chunk), part.dtype),
+            dma((1,)),
+        ]
+        + [dma((far_count,))] * 2
+        + [dma((CHUNKS,))] * 4
+        + [dma((n - 1,))] * 2,
+        compiler_params=pltpu.CompilerParams(
+            collective_id=1, has_side_effects=True, vmem_limit_bytes=32 * 1024 * 1024
+        ),
+    )(part, grad)
 
 
 def on_device(preactivations, route_weights, expert_ids, down_proj, output_cotangent):
@@ -27,25 +263,39 @@
     weighted = (slot_weight * hidden).astype(jnp.bfloat16)
     weight = down_proj[0]
 
-    cot_rows = lax.all_gather(output_cotangent, "expert", axis=0, tiled=True)
     send = jnp.dot(placement, weighted, preferred_element_type=jnp.float32).astype(jnp.bfloat16)
     send = send.reshape(experts, token_count, hidden_units)
-    recv = lax.all_to_all(send, "expert", split_axis=0, concat_axis=0, tiled=True)
-    hidden_rows = recv.reshape(experts * token_count, hidden_units)
-
-    mixed_part = lax.dot_general(
-        hidden_rows, weight, (((1,), (1,)), ((), ())), preferred_element_type=jnp.float32
-    ).astype(jnp.bfloat16)
-    mixed = lax.psum_scatter(mixed_part, "expert", scatter_dimension=0, tiled=True)
-
-    grad_rows = jnp.dot(cot_rows, weight, preferred_element_type=jnp.float32).astype(jnp.bfloat16)
-    grad_back = lax.all_to_all(
-        grad_rows.reshape(experts, token_count, hidden_units),
-        "expert",
-        split_axis=0,
-        concat_axis=0,
-        tiled=True,
-    ).reshape(experts * token_count, hidden_units)
+    by_kernel = copies == 2 and experts % 4 == 0 and experts > 4
+    rows = experts * token_count
+    if by_kernel:
+        cot_rows, recv = spread(output_cotangent, send)
+        cot_rows = cot_rows.reshape(rows, model_width)
+    else:
+        cot_rows = lax.all_gather(output_cotangent, "expert", axis=0, tiled=True)
+        recv = lax.all_to_all(send, "expert", split_axis=0, concat_axis=0, tiled=True)
+    hidden_rows = recv.reshape(rows, hidden_units)
+    grad_rows = (
+        jnp.dot(cot_rows, weight, preferred_element_type=jnp.float32)
+        .astype(jnp.bfloat16)
+        .reshape(experts, token_count, hidden_units)
+    )
+    across = (((1,), (1,)), ((), ()))
+    if by_kernel:
+        ordered = recv.reshape(experts // 4, 2, 2, token_count, hidden_units)
+        ordered = ordered.transpose(2, 1, 0, 3, 4)
+        mixed_part = lax.dot_general(
+            ordered.reshape(rows, hidden_units), weight, across, preferred_element_type=jnp.float32
+        ).astype(jnp.bfloat16)
+        mixed, grad_back = collect(
+            mixed_part.reshape(2, 2, experts // 4, token_count, model_width), grad_rows
+        )
+    else:
+        mixed_part = lax.dot_general(
+            hidden_rows, weight, across, preferred_element_type=jnp.float32
+        ).astype(jnp.bfloat16)
+        mixed = lax.psum_scatter(mixed_part, "expert", scatter_dimension=0, tiled=True)
+        grad_back = lax.all_to_all(grad_rows, "expert", split_axis=0, concat_axis=0, tiled=True)
+    grad_back = grad_back.reshape(rows, hidden_units)
 
     if copies == 2:
         half = model_width // 2

time: 128 us -> 84.8 us (0.66)
  Pallas kernels: 0 us -> 58.7 us
  waiting for transfers between devices: 55.2 us -> 0.01 us
  blocking collectives: 22.4 us -> 0 us
  between operations: 14.1 us -> 0.81 us
  matrix products: 25 us -> 15.8 us
  starting transfers between devices: 6.37 us -> 2.05 us
  local copies, waits for them, and re-layouts: 2.4 us -> 4.51 us
    pallas_call x0 -> x2, Pallas kernels: none -> 58.7 us  [the longest x1 31.6 us: collect(): pl.pallas_call(functools.partial(collect_kernel, n), out_shape=(jax.Shape...]
    all_to_all x1 -> x0, blocking collectives: 22.4 us -> none  [on_device(): lax.all_to_all(send, 'expert', split_axis=0, concat_axis=0, tiled=True)]
    ppermute x1, waiting for transfers between devices: 18.6 us -> 0.01 us  [on_device(): hidden_other = lax.ppermute(hidden_rows, 'dp', swap)]
    all_gather x1 -> x0, waiting for transfers between devices: 16.4 us -> none  [on_device(): cot_rows = lax.all_gather(output_cotangent, 'expert', axis=0, tiled=True)]
    reduce_scatter x1 -> x0, waiting for transfers between devices: 13.3 us -> none  [on_device(): lax.psum_scatter(mixed_part, 'expert', scatter_dimension=0, tiled=True)]
    all_to_all x1 -> x0, waiting for transfers between devices: 6.24 us -> none  [on_device(): lax.all_to_all(grad_rows.reshape(experts, token_count, hidden_units), 'ex...]
    all_to_all x1 -> x0, starting transfers between devices: 4.21 us -> none  [on_device(): lax.all_to_all(grad_rows.reshape(experts, token_count, hidden_units), 'ex...]
    dot_general x1, matrix products: 6.02 us -> 1.82 us  [on_device(): lax.dot_general(ordered.reshape(rows, hidden_units), weight, across, pref...]
  transfers between devices with their start and end apart: 5 -> 2, of which waited for: 4 -> 0; matrix products, arithmetic and copies ran while one was open for 23% -> 14% of each run, Pallas kernels for 0% -> 37%
where the time goes in v2:
time: 84.8 us; the launch traced here: 84.4 us
  Pallas kernels  58.7 us (69%)
  matrix products  15.8 us (19%)
  local copies, waits for them, and re-layouts  4.51 us (5%)
  other arithmetic  2.56 us (3%)
  starting transfers between devices  2.05 us (2%)
    pallas_call x1, Pallas kernels, collect(): pl.pallas_call(functools.partial(collect_kernel, n), out_shape=(jax.Shape...  31.6 us
    pallas_call x1, Pallas kernels, spread(): pl.pallas_call(functools.partial(spread_kernel, n), out_shape=(jax.ShapeD...  27.1 us
    dot_general x1, matrix products, on_device(): lax.dot_general(cot_other, hidden_other, contract, preferred_element_type...  5.04 us
    dot_general x1, matrix products, on_device(): jnp.dot(cot_rows, weight, preferred_element_type=jnp.float32)  4.71 us
    unnamed x13, local copies, waits for them, and re-layouts  3.02 us
    dot_general x1, matrix products, on_device(): lax.dot_general(cot_keep, hidden_rows, contract, preferred_element_type=j...  2.25 us
    dot_general x1, matrix products, on_device(): lax.dot_general(ordered.reshape(rows, hidden_units), weight, across, pref...  1.82 us
  transfers between devices with their start and end apart: 2, of which 0 were waited for; matrix products, arithmetic and copies ran while one was open for 14% of the time, Pallas kernels for 37%

profile of v2, /device:TPU:0, one launch (start us, length us, event | category | flops | bytes accessed | tf_op | source)
XLA Modules:
  0.0 84.4 jit_solution(10487872587114991340)
XLA Ops:
  0.6 0.8 copy.13
  1.4 0.1 mul.62
  1.5 1.1 %bitcast_convert_fusion = f32[128,1536]{1,0:T(8,128)S(1)} fusion(bf16[16,8,1536]{2,1,0:T(8,128)(2,1)} %param.5), kind=kLoop, calls=%fused_computation.11 | loop fusion | flops 196608 | bytes 1179648 | tf_op jit(solution)/shard_map/convert_element_type | solution.py:256
  2.6 0.0 copy-start.2
  2.6 0.7 broadcast_multiply_fusion
  3.3 0.1 copy.12
  3.4 0.1 mul.61
  3.5 0.4 convolution_convert_fusion
  3.8 0.0 copy-done.2
  3.8 0.0 copy-start.1
  3.8 0.9 %copy-done.1 = bf16[16,4096]{1,0:T(8,128)(2,1)S(1)} copy-done((bf16[16,4096]{1,0:T(8,128)(2,1)S(1)}, bf16[16,4096]{1,0:T(8,128)(2,1)}, u32[]{:S(2)}) %copy-start.1) | copy-done | bytes 131096
  4.7 27.1 %shard_map.84 = (bf16[16,16,4096]{2,1,0:T(8,128)(2,1)S(1)}, bf16[16,16,768]{2,1,0:T(8,128)(2,1)S(1)}) custom-call(bf16[16,4096]{1,0:T(8,128)(2,1)S(1)} %copy-done.1, bf16[16,16,768]{2,1,0:T(8,128)(2,1)S(1)} %bitcast.42), custom_call_target="tpu_custom_call" | custom-call | tf_op jit(solution)/shard_map/pallas_call | solution.py:102
  31.9 0.0 copy-start
  31.9 1.1 %constant_dynamic-slice_fusion = bf16[256,2048]{1,0:T(8,128)(2,1)} fusion(bf16[256,4096]{1,0:T(8,128)(2,1)S(1)} %bitcast.35, s32[]{:T(128)S(6)} %select_n.17), kind=kLoop, calls=%fused_computation.32 | loop fusion | bytes 2097156 | tf_op jit(solution)/shard_map/dynamic_slice | solution.py:305
  33.0 1.5 %collective-permute-start = (bf16[256,2048]{1,0:T(8,128)(2,1)}, bf16[256,2048]{1,0:T(8,128)(2,1)}, u32[]{:S(2)}, u32[]{:S(2)}) collective-permute-start(bf16[256,2048]{1,0:T(8,128)(2,1)} %constant_dynamic-slice_fusion), channel_id=1, source_target_pairs={{0,16},{16,0},{1,17},{17,1},{2,18},{18,2},{3,19},{19,3},{4,20},{20... | collective-permute-start | bytes 3145736 | tf_op jit(solution)/shard_map/ppermute | solution.py:306
  34.5 0.5 collective-permute-start.1
  35.1 0.0 slice-start
  35.1 0.0 slice-start.1
  35.1 4.7 %fusion.7 = bf16[256,768]{1,0:T(8,128)(2,1)S(1)} fusion(bf16[256,4096]{1,0:T(8,128)(2,1)S(1)} %bitcast.36, bf16[1,4096,768]{2,1,0:T(8,128)(2,1)} %param.8), kind=kOutput, calls=%fused_computation.7 | convolution fusion | flops 1610809344 | bytes 8781824 | tf_op jit(solution)/shard_map/dot_general | solution.py:278
  39.9 0.0 copy-done
  39.9 0.0 slice-done
  39.9 0.0 slice-done.1
  39.9 1.8 %fusion.4 = bf16[256,4096]{1,0:T(8,128)(2,1)S(1)} fusion(bf16[256,768]{1,0:T(8,128)(2,1)S(1)} %bitcast.44, bf16[1,4096,768]{2,1,0:T(8,128)(2,1)S(1)} %bitcast.46), kind=kOutput, calls=%fused_computation.5 | convolution fusion | flops 1611661312 | bytes 8781824 | tf_op jit(solution)/shard_map/dot_general | solution.py:286
  41.7 31.6 %shard_map.85 = (bf16[16,4096]{1,0:T(8,128)(2,1)S(1)}, bf16[16,16,768]{2,1,0:T(8,128)(2,1)S(1)}) custom-call(bf16[2,2,4,16,4096]{4,3,2,1,0:T(8,128)(2,1)S(1)} %bitcast.34, bf16[16,16,768]{2,1,0:T(8,128)(2,1)S(1)} %bitcast.41), custom_call_target="tpu_custom_call" | custom-call | tf_op jit(solution)/shard_map/pallas_call | solution.py:218
  73.3 1.6 %fusion.15 = (bf16[16,8,768]{2,1,0:T(8,128)(2,1)S(1)}, bf16[16,8,768]{2,1,0:T(8,128)(2,1)S(1)}, f32[128]{0:T(128)S(1)}) fusion(f32[128,1536]{1,0:T(8,128)} %copy-done.2, f32[128]{0:T(128)S(1)} %mul.62, bf16[256,768]{1,0:T(8,128)(2,1)S(1)} %bitcast.43, s32[128]{0:T(128)S(1)} %fusion.19), kind=kOutput, calls=%fused_computation.21 | convolution fusion | flops 52035456 | bytes 1574400 | tf_op jit(solution)/shard_map/dot_general | solution.py:324
  74.9 0.1 reshape.74
  75.0 0.7 copy.15
  75.7 0.8 pad_maximum_fusion
  76.5 2.3 %fusion.10 = f32[2048,768]{1,0:T(8,128)S(1)} fusion(bf16[256,768]{1,0:T(8,128)(2,1)S(1)} %bitcast.40, bf16[256,4096]{1,0:T(8,128)(2,1)} %bitcast.37, s32[]{:T(128)S(6)} %select_n.16), kind=kOutput, calls=%fused_computation.8 | convolution fusion | flops 805306368 | bytes 7733252 | tf_op jit(solution)/shard_map/dot_general | solution.py:309
  78.7 0.0 collective-permute-done.1
  78.7 0.0 collective-permute-done
  78.7 5.0 %add_bitcast_fusion = f32[1,2048,768]{2,1,0:T(8,128)} fusion(f32[2048,768]{1,0:T(8,128)S(1)} %fusion.10, bf16[256,2048]{1,0:T(8,128)(2,1)} %collective-permute-done, bf16[256,768]{1,0:T(8,128)(2,1)S(1)} %collective-permute-done.1), kind=kOutput, calls=%fused_computation.4 | convolution fusion | flops 806879232 | bytes 14024704 | tf_op jit(solution)/shard_map/dot_general | solution.py:311
  83.8 0.7 copy.17
  (3 shorter events, 0.0 us)
Async XLA Ops:
  2.6 1.3 %copy-start.2 = (f32[128,1536]{1,0:T(8,128)}, f32[128,1536]{1,0:T(8,128)S(1)}, u32[]{:S(2)}) copy-start(f32[128,1536]{1,0:T(8,128)S(1)} %bitcast_convert_fusion) | copy-start | bytes 2359300
  3.8 0.9 %copy-start.1 = (bf16[16,4096]{1,0:T(8,128)(2,1)S(1)}, bf16[16,4096]{1,0:T(8,128)(2,1)}, u32[]{:S(2)}) copy-start(bf16[16,4096]{1,0:T(8,128)(2,1)} %cot_ref.1) | copy-start | bytes 393220
  31.9 8.0 %copy-start = (bf16[16,16,4096]{2,1,0:T(8,128)(2,1)}, bf16[16,16,4096]{2,1,0:T(8,128)(2,1)S(1)}, u32[]{:S(2)}) copy-start(bf16[16,16,4096]{2,1,0:T(8,128)(2,1)S(1)} %get-tuple-element.9) | copy-start | bytes 6291460
  33.0 45.7 %collective-permute-start = (bf16[256,2048]{1,0:T(8,128)(2,1)}, bf16[256,2048]{1,0:T(8,128)(2,1)}, u32[]{:S(2)}, u32[]{:S(2)}) collective-permute-start(bf16[256,2048]{1,0:T(8,128)(2,1)} %constant_dynamic-slice_fusion), channel_id=1, source_target_pairs={{0,16},{16,0},{1,17},{17,1},{2,18},{18,2},{3,19},{19,3},{4,20},{20... | collective-permute-start | bytes 3145736 | tf_op jit(solution)/shard_map/ppermute | solution.py:306
  34.5 44.2 %collective-permute-start.1 = (bf16[256,768]{1,0:T(8,128)(2,1)S(1)}, bf16[256,768]{1,0:T(8,128)(2,1)S(1)}, u32[]{:S(2)}, u32[]{:S(2)}) collective-permute-start(bf16[256,768]{1,0:T(8,128)(2,1)S(1)} %bitcast.38), channel_id=1, source_target_pairs={{0,16},{16,0},{1,17},{17,1},{2,18},{18,2},{3,19},{19,3},{4,20},{20... | collective-permute-start | bytes 1179656 | tf_op jit(solution)/shard_map/ppermute | solution.py:307
  35.1 4.8 %slice-start = ((s8[6291456]{0:T(1024)(128)(4,1)}), s8[4194304]{0:T(1024)(128)(4,1)S(1)}, s32[]{:S(2)}) async-start(s8[6291456]{0:T(1024)(128)(4,1)} %bitcast.45), calls=%async_computation | async-start | bytes 8388608
  35.1 4.8 %slice-start.1 = ((s8[6291456]{0:T(1024)(128)(4,1)}), s8[2097152]{0:T(1024)(128)(4,1)S(1)}, s32[]{:S(2)}) async-start(s8[6291456]{0:T(1024)(128)(4,1)} %bitcast.45), calls=%async_computation.1 | async-start | bytes 4194304

commit v3 on v1

--- a/solution.py
+++ b/solution.py
@@ -1,7 +1,290 @@
+import functools
+
 import jax
 import jax.numpy as jnp
 from jax import lax
+from jax.experimental import pallas as pl
+from jax.experimental.pallas import tpu as pltpu
 from jax.sharding import PartitionSpec as P
+
+MESH = pl.DeviceIdType.MESH
+CHUNKS = 4
+
+
+def place(n):
+    me = lax.axis_index("expert")
+    return me, me // 4, (me // 2) % 2, me % 2, n // 4
+
+
+def greet(n):
+    me = lax.axis_index("expert")
+    barrier = pltpu.get_barrier_semaphore()
+    for step in range(1, n):
+        pl.semaphore_signal(
+            barrier, inc=1, device_id={"expert": (me + step) % n}, device_id_type=MESH
+        )
+    pl.semaphore_signal(
+        barrier, inc=1, device_id={"dp": 1 - lax.axis_index("dp")}, device_id_type=MESH
+    )
+    pl.semaphore_wait(barrier, n)
+
+
+def layer_kernel(
+    n,
+    cot_ref,
+    send_ref,
+    weight_ref,
+    cot_all,
+    recv_all,
+    mixed_ref,
+    back_ref,
+    cot_far,
+    recv_far,
+    *scratch,
+):
+    held, part, grad, core_buf, core_sum, near_buf, near_sum, far_buf = scratch[:8]
+    own_sem, far_s, far_r, near_s, near_r, core_s, core_r, swap_s, swap_r = scratch[8:17]
+    ofar_s, ofar_r, onear_s, onear_r, ocore_s, ocore_r, oswap_s, oswap_r = scratch[17:25]
+    pair_s, pair_r, pass_s, pass_r = scratch[25:]
+    me, far, near, core, fars = place(n)
+    tokens, width = cot_ref.shape
+    hidden_units = send_ref.shape[-1]
+    chunk = width // CHUNKS
+
+    def remote(src, dst, send_sem, recv_sem, target):
+        copy = pltpu.make_async_remote_copy(
+            src_ref=src,
+            dst_ref=dst,
+            send_sem=send_sem,
+            recv_sem=recv_sem,
+            device_id={"expert": target},
+            device_id_type=MESH,
+        )
+        copy.start()
+        return copy
+
+    half = width // 2
+    other = 1 - lax.axis_index("dp")
+    columns_there = pl.ds(pl.multiple_of(other * half, half), half)
+
+    def pair(src, dst, at):
+        copy = pltpu.make_async_remote_copy(
+            src_ref=src,
+            dst_ref=dst,
+            send_sem=pair_s.at[at],
+            recv_sem=pair_r.at[at],
+            device_id={"dp": other},
+            device_id_type=MESH,
+        )
+        copy.start()
+        return copy
+
+    def added(left, right):
+        return (left.astype(jnp.float32) + right.astype(jnp.float32)).astype(jnp.bfloat16)
+
+    keep_cot = pltpu.make_async_copy(cot_ref, cot_all.at[me], own_sem.at[0])
+    keep_row = pltpu.make_async_copy(send_ref.at[me], recv_all.at[me], own_sem.at[1])
+    load = pltpu.make_async_copy(weight_ref, held, own_sem.at[2])
+    keep_cot.start()
+    keep_row.start()
+    load.start()
+    greet(n)
+    sibling = me + 1 - 2 * core
+    beside = me + 2 - 4 * near
+
+    swap_copies = []
+    for step in range(1, n):
+        target = (me + step) % n
+        swap_copies.append(
+            remote(
+                send_ref.at[target],
+                recv_all.at[me],
+                swap_s.at[step - 1],
+                swap_r.at[step - 1],
+                target,
+            )
+        )
+    far_copies = [
+        remote(
+            cot_ref,
+            cot_all.at[me],
+            far_s.at[step - 1],
+            far_r.at[step - 1],
+            ((far + step) % fars) * 4 + near * 2 + core,
+        )
+        for step in range(1, fars)
+    ]
+    near_copies = [remote(cot_ref, cot_all.at[me], near_s.at[0], near_r.at[0], beside)]
+    core_copies = [remote(cot_ref, cot_all.at[me], core_s.at[0], core_r.at[0], sibling)]
+    blocks = [me]
+    pairs = [pair(cot_ref.at[:, columns_there], cot_far.at[me], 0)]
+    for step in range(1, fars):
+        far_copies[step - 1].wait_recv()
+        block = ((far - step + fars) % fars) * 4 + near * 2 + core
+        ref = cot_all.at[block]
+        near_copies.append(remote(ref, ref, near_s.at[step], near_r.at[step], beside))
+        core_copies.append(remote(ref, ref, core_s.at[step], core_r.at[step], sibling))
+        pairs.append(pair(ref.at[:, columns_there], cot_far.at[block], step))
+        blocks.append(block)
+
+    for copy in swap_copies:
+        copy.wait_recv()
+    keep_row.wait()
+    row_pair = pair(recv_all, recv_far, 2 * fars)
+    load.wait()
+    hidden = recv_all[...].reshape(n * tokens, hidden_units)
+    ocore = []
+    for at in range(CHUNKS):
+        out = lax.dot_general(
+            hidden,
+            held[at * chunk : (at + 1) * chunk, :],
+            (((1,), (1,)), ((), ())),
+            preferred_element_type=jnp.float32,
+        )
+        part[at] = out.astype(jnp.bfloat16).reshape(fars, 2, 2, tokens, chunk)
+        ocore.append(
+            remote(
+                part.at[at, :, :, 1 - core],
+                core_buf.at[at],
+                ocore_s.at[at],
+                ocore_r.at[at],
+                sibling,
+            )
+        )
+
+    for step in range(fars):
+        near_copies[step].wait_recv()
+        block = ((far - step + fars) % fars) * 4 + (1 - near) * 2 + core
+        ref = cot_all.at[block]
+        at = fars + step
+        core_copies.append(remote(ref, ref, core_s.at[at], core_r.at[at], sibling))
+        pairs.append(pair(ref.at[:, columns_there], cot_far.at[block], at))
+        blocks.append(block)
+
+    onear = []
+    for at in range(CHUNKS):
+        ocore[at].wait_recv()
+        core_sum[at] = added(part[at, :, :, core], core_buf[at])
+        onear.append(
+            remote(
+                core_sum.at[at, :, 1 - near],
+                near_buf.at[at],
+                onear_s.at[at],
+                onear_r.at[at],
+                beside,
+            )
+        )
+
+    for copy in core_copies:
+        copy.wait_recv()
+    keep_cot.wait()
+    tile = hidden_units // 3 if hidden_units % 384 == 0 else hidden_units
+
+    @pl.loop(0, hidden_units // tile)
+    def _(at):
+        columns = pl.ds(pl.multiple_of(at * tile, tile), tile)
+        found = jnp.dot(
+            cot_all[...].reshape(n * tokens, width),
+            held[:, columns],
+            preferred_element_type=jnp.float32,
+        )
+        grad[:, :, columns] = found.astype(jnp.bfloat16).reshape(n, tokens, tile)
+
+    keep_grad = pltpu.make_async_copy(grad.at[me], back_ref.at[me], own_sem.at[3])
+    keep_grad.start()
+    oswap = []
+    for step in range(1, n):
+        target = (me + step) % n
+        oswap.append(
+            remote(
+                grad.at[target],
+                back_ref.at[me],
+                oswap_s.at[step - 1],
+                oswap_r.at[step - 1],
+                target,
+            )
+        )
+    ofar = []
+    for at in range(CHUNKS):
+        onear[at].wait_recv()
+        near_sum[at] = added(core_sum[at, :, near], near_buf[at])
+        for step in range(1, fars):
+            target = (far + step) % fars
+            slot = at * (fars - 1) + step - 1
+            ofar.append(
+                remote(
+                    near_sum.at[at, target],
+                    far_buf.at[at, step - 1],
+                    ofar_s.at[slot],
+                    ofar_r.at[slot],
+                    target * 4 + near * 2 + core,
+                )
+            )
+    for at in range(CHUNKS):
+        for step in range(1, fars):
+            ofar[at * (fars - 1) + step - 1].wait_recv()
+        total = near_sum[at, far].astype(jnp.float32)
+        for step in range(1, fars):
+            total = total + far_buf[at, step - 1].astype(jnp.float32)
+        mixed_ref[:, at * chunk : (at + 1) * chunk] = total.astype(jnp.bfloat16)
+    passes = []
+    for at in range(2 * fars):
+        pairs[at].wait_recv()
+        ref = cot_far.at[blocks[at]]
+        passes.append(remote(ref, ref, pass_s.at[at], pass_r.at[at], sibling))
+    for copy in oswap + passes + [row_pair]:
+        copy.wait_recv()
+    for copy in far_copies + near_copies + core_copies + swap_copies:
+        copy.wait_send()
+    for copy in ocore + onear + ofar + oswap + pairs + passes + [row_pair]:
+        copy.wait_send()
+    keep_grad.wait()
+
+
+def layer(cot, send, weight):
+    n, tokens, hidden_units = send.shape
+    width = cot.shape[1]
+    chunk = width // CHUNKS
+    fars = n // 4
+    kind = cot.dtype
+    dma = pltpu.SemaphoreType.DMA
+    in_vmem = pl.BlockSpec(memory_space=pltpu.VMEM)
+    return pl.pallas_call(
+        functools.partial(layer_kernel, n),
+        out_shape=(
+            jax.ShapeDtypeStruct((n, tokens, width), kind),
+            jax.ShapeDtypeStruct((n, tokens, hidden_units), kind),
+            jax.ShapeDtypeStruct((tokens, width), kind),
+            jax.ShapeDtypeStruct((n, tokens, hidden_units), kind),
+            jax.ShapeDtypeStruct((n, tokens, width // 2), kind),
+            jax.ShapeDtypeStruct((n, tokens, hidden_units), kind),
+        ),
+        in_specs=[in_vmem, in_vmem, pl.BlockSpec(memory_space=pltpu.HBM)],
+        out_specs=[in_vmem] * 6,
+        scratch_shapes=[
+            pltpu.VMEM(weight.shape, kind),
+            pltpu.VMEM((CHUNKS, fars, 2, 2, tokens, chunk), kind),
+            pltpu.VMEM((n, tokens, hidden_units), kind),
+            pltpu.VMEM((CHUNKS, fars, 2, tokens, chunk), kind),
+            pltpu.VMEM((CHUNKS, fars, 2, tokens, chunk), kind),
+            pltpu.VMEM((CHUNKS, fars, tokens, chunk), kind),
+            pltpu.VMEM((CHUNKS, fars, tokens, chunk), kind),
+            pltpu.VMEM((CHUNKS, fars - 1, tokens, chunk), kind),
+            dma((4,)),
+        ]
+        + [dma((fars - 1,))] * 2
+        + [dma((fars,))] * 2
+        + [dma((2 * fars,))] * 2
+        + [dma((n - 1,))] * 2
+        + [dma((CHUNKS * (fars - 1),))] * 2
+        + [dma((CHUNKS,))] * 4
+        + [dma((n - 1,))] * 2
+        + [dma((2 * fars + 1,))] * 2
+        + [dma((2 * fars,))] * 2,
+        compiler_params=pltpu.CompilerParams(
+            collective_id=0, has_side_effects=True, vmem_limit_bytes=40 * 1024 * 1024
+        ),
+    )(cot, send, weight)
 
 
 def on_device(preactivations, route_weights, expert_ids, down_proj, output_cotangent):
@@ -27,34 +310,37 @@
     weighted = (slot_weight * hidden).astype(jnp.bfloat16)
     weight = down_proj[0]
 
-    cot_rows = lax.all_gather(output_cotangent, "expert", axis=0, tiled=True)
     send = jnp.dot(placement, weighted, preferred_element_type=jnp.float32).astype(jnp.bfloat16)
     send = send.reshape(experts, token_count, hidden_units)
-    recv = lax.all_to_all(send, "expert", split_axis=0, concat_axis=0, tiled=True)
-    hidden_rows = recv.reshape(experts * token_count, hidden_units)
-
-    mixed_part = lax.dot_general(
-        hidden_rows, weight, (((1,), (1,)), ((), ())), preferred_element_type=jnp.float32
-    ).astype(jnp.bfloat16)
-    mixed = lax.psum_scatter(mixed_part, "expert", scatter_dimension=0, tiled=True)
-
-    grad_rows = jnp.dot(cot_rows, weight, preferred_element_type=jnp.float32).astype(jnp.bfloat16)
-    grad_back = lax.all_to_all(
-        grad_rows.reshape(experts, token_count, hidden_units),
-        "expert",
-        split_axis=0,
-        concat_axis=0,
-        tiled=True,
-    ).reshape(experts * token_count, hidden_units)
-
-    if copies == 2:
+    by_kernel = copies == 2 and experts % 4 == 0 and experts > 4
+    rows = experts * token_count
+    if by_kernel:
+        cot_rows, recv, mixed, grad_back, cot_other, hidden_other = layer(
+            output_cotangent, send, weight
+        )
+        cot_other = cot_other.reshape(rows, model_width // 2)
+        hidden_other = hidden_other.reshape(rows, hidden_units)
+        cot_rows = cot_rows.reshape(rows, model_width)
+        hidden_rows = recv.reshape(rows, hidden_units)
+    else:
+        cot_rows = lax.all_gather(output_cotangent, "expert", axis=0, tiled=True)
+        recv = lax.all_to_all(send, "expert", split_axis=0, concat_axis=0, tiled=True)
+        hidden_rows = recv.reshape(rows, hidden_units)
+        grad_rows = (
+            jnp.dot(cot_rows, weight, preferred_element_type=jnp.float32)
+            .astype(jnp.bfloat16)
+            .reshape(experts, token_count, hidden_units)
+        )
+        mixed_part = lax.dot_general(
+            hidden_rows, weight, (((1,), (1,)), ((), ())), preferred_element_type=jnp.float32
+        ).astype(jnp.bfloat16)
+        mixed = lax.psum_scatter(mixed_part, "expert", scatter_dimension=0, tiled=True)
+        grad_back = lax.all_to_all(grad_rows, "expert", split_axis=0, concat_axis=0, tiled=True)
+    grad_back = grad_back.reshape(rows, hidden_units)
+
+    if by_kernel:
         half = model_width // 2
-        mine = lax.axis_index("dp")
-        swap = [(0, 1), (1, 0)]
-        cot_keep = lax.dynamic_slice_in_dim(cot_rows, mine * half, half, 1)
-        cot_give = lax.dynamic_slice_in_dim(cot_rows, (1 - mine) * half, half, 1)
-        cot_other = lax.ppermute(cot_give, "dp", swap)
-        hidden_other = lax.ppermute(hidden_rows, "dp", swap)
+        cot_keep = lax.dynamic_slice_in_dim(cot_rows, lax.axis_index("dp") * half, half, 1)
         contract = (((0,), (0,)), ((), ()))
         weight_grads = lax.dot_general(
             cot_keep, hidden_rows, contract, preferred_element_type=jnp.float32

time: 128 us -> 78.8 us (0.62)
  Pallas kernels: 0 us -> 62.3 us
  waiting for transfers between devices: 55.2 us -> 0 us
  blocking collectives: 22.4 us -> 0 us
  matrix products: 25 us -> 5.67 us
  between operations: 14.1 us -> 0.7 us
  starting transfers between devices: 6.37 us -> 0 us
  local copies, waits for them, and re-layouts: 2.4 us -> 7.24 us
    pallas_call x0 -> x1, Pallas kernels: none -> 62.3 us  [layer(): pl.pallas_call(functools.partial(layer_kernel, n), out_shape=(jax.ShapeDt...]
    all_to_all x1 -> x0, blocking collectives: 22.4 us -> none  [on_device(): lax.all_to_all(send, 'expert', split_axis=0, concat_axis=0, tiled=True)]
    ppermute x2 -> x0, waiting for transfers between devices: 18.6 us -> none  [the longest x1 18.6 us: on_device(): hidden_other = lax.ppermute(hidden_rows, 'dp', swap)]
    all_gather x1 -> x0, waiting for transfers between devices: 16.4 us -> none  [on_device(): cot_rows = lax.all_gather(output_cotangent, 'expert', axis=0, tiled=True)]
    reduce_scatter x1 -> x0, waiting for transfers between devices: 13.3 us -> none  [on_device(): lax.psum_scatter(mixed_part, 'expert', scatter_dimension=0, tiled=True)]
    dot_general x2 -> x0, matrix products: 12.1 us -> none  [the longest x1 6.09 us: on_device(): jnp.dot(cot_rows, weight, preferred_element_type=jnp.float32)]
    all_to_all x1 -> x0, waiting for transfers between devices: 6.24 us -> none  [on_device(): lax.all_to_all(grad_rows.reshape(experts, token_count, hidden_units), 'ex...]
    unnamed x6 -> x11, local copies, waits for them, and re-layouts: 1.97 us -> 6.92 us
  transfers between devices with their start and end apart: 5 -> 0, of which waited for: 4 -> 0; matrix products, arithmetic and copies ran while one was open for 23% -> 0% of each run, Pallas kernels for 0% -> 0%
where the time goes in v3:
time: 78.8 us; the launch traced here: 78.5 us
  Pallas kernels  62.3 us (79%)
  local copies, waits for them, and re-layouts  7.24 us (9%)
  matrix products  5.67 us (7%)
  other arithmetic  2.54 us (3%)
    pallas_call x1, Pallas kernels, layer(): pl.pallas_call(functools.partial(layer_kernel, n), out_shape=(jax.ShapeDt...  62.3 us
    unnamed x11, local copies, waits for them, and re-layouts  6.92 us
    dot_general x1, matrix products, on_device(): lax.dot_general(cot_other, hidden_other, contract, preferred_element_type...  3.82 us

profile of v3, /device:TPU:0, one launch (start us, length us, event | category | flops | bytes accessed | tf_op | source)
XLA Modules:
  0.0 78.5 jit_solution(16038740618573443625)
XLA Ops:
  0.6 0.7 broadcast_multiply_fusion
  1.3 0.1 copy.12
  1.4 0.1 mul.58
  1.5 0.8 copy.13
  2.3 0.1 mul.59
  2.4 1.1 %bitcast_convert_fusion = f32[128,1536]{1,0:T(8,128)S(1)} fusion(bf16[16,8,1536]{2,1,0:T(8,128)(2,1)} %param.5), kind=kLoop, calls=%fused_computation.6 | loop fusion | flops 196608 | bytes 1179648 | tf_op jit(solution)/shard_map/convert_element_type | solution.py:303
  3.4 0.4 convolution_convert_fusion
  3.8 0.0 copy-start
  3.8 2.8 %copy-done = bf16[1,4096,768]{2,1,0:T(8,128)(2,1)S(1)} copy-done((bf16[1,4096,768]{2,1,0:T(8,128)(2,1)S(1)}, bf16[1,4096,768]{2,1,0:T(8,128)(2,1)}, u32[]{:S(2)}) %copy-start) | copy-done | bytes 6291480
  6.6 0.0 copy-start.1
  6.6 0.9 %copy-done.1 = bf16[16,4096]{1,0:T(8,128)(2,1)S(1)} copy-done((bf16[16,4096]{1,0:T(8,128)(2,1)S(1)}, bf16[16,4096]{1,0:T(8,128)(2,1)}, u32[]{:S(2)}) %copy-start.1) | copy-done | bytes 131096
  7.5 62.3 %shard_map.84 = (bf16[16,16,4096]{2,1,0:T(8,128)(2,1)S(1)}, bf16[16,16,768]{2,1,0:T(8,128)(2,1)S(1)}, bf16[16,4096]{1,0:T(8,128)(2,1)S(1)}, bf16[16,16,768]{2,1,...) custom-call(bf16[16,4096]{1,0:T(8,128)(2,1)S(1)} %copy-done.1, ...), custom_call_target="tpu_custom_call" | custom-call | tf_op jit(solution)/shard_map/pallas_call | solution.py:252
  69.8 0.0 copy-start.2
  69.8 1.0 %copy-done.2 = bf16[16,16,2048]{2,1,0:T(8,128)(2,1)} copy-done((bf16[16,16,2048]{2,1,0:T(8,128)(2,1)}, bf16[16,16,2048]{2,1,0:T(8,128)(2,1)S(1)}, u32[]{:S(2)}) %copy-start.2) | copy-done | bytes 1048600
  70.8 0.5 fusion.6
  71.2 0.8 pad_maximum_fusion
  72.0 0.1 reshape.59
  72.1 0.7 copy.14
  72.8 0.0 copy-start.3
  72.8 1.0 %fusion.1 = f32[2048,768]{1,0:T(8,128)S(1)} fusion(bf16[256,768]{1,0:T(8,128)(2,1)S(1)} %bitcast.24, bf16[256,4096]{1,0:T(8,128)(2,1)S(1)} %bitcast.23, s32[]{:T(128)S(6)} %select_n.13), kind=kOutput, calls=%fused_computation.3 | convolution fusion | flops 805306368 | bytes 7733252 | tf_op jit(solution)/shard_map/dot_general | solution.py:345
  73.8 0.2 copy-done.3
  74.0 3.8 %fusion = f32[1,2048,768]{2,1,0:T(8,128)} fusion(f32[2048,768]{1,0:T(8,128)S(1)} %fusion.1, bf16[16,16,2048]{2,1,0:T(8,128)(2,1)S(1)} %copy-done.3, bf16[16,16,768]{2,1,0:T(8,128)(2,1)S(1)} %get-tuple-element.15), kind=kOutput, calls=%fused_computation.1 | convolution fusion | flops 806879232 | bytes 14024704 | tf_op jit(solution)/shard_map/dot_general | solution.py:347
  77.8 0.7 copy.16
  (1 shorter events, 0.0 us)
Async XLA Ops:
  3.8 2.8 %copy-start = (bf16[1,4096,768]{2,1,0:T(8,128)(2,1)S(1)}, bf16[1,4096,768]{2,1,0:T(8,128)(2,1)}, u32[]{:S(2)}) copy-start(bf16[1,4096,768]{2,1,0:T(8,128)(2,1)} %param.8) | copy-start | bytes 18874372
  6.6 0.9 %copy-start.1 = (bf16[16,4096]{1,0:T(8,128)(2,1)S(1)}, bf16[16,4096]{1,0:T(8,128)(2,1)}, u32[]{:S(2)}) copy-start(bf16[16,4096]{1,0:T(8,128)(2,1)} %cot_ref.1) | copy-start | bytes 393220
  69.8 1.0 %copy-start.2 = (bf16[16,16,2048]{2,1,0:T(8,128)(2,1)}, bf16[16,16,2048]{2,1,0:T(8,128)(2,1)S(1)}, u32[]{:S(2)}) copy-start(bf16[16,16,2048]{2,1,0:T(8,128)(2,1)S(1)} %get-tuple-element.14) | copy-start | bytes 3145732
  72.8 1.2 %copy-start.3 = (bf16[16,16,2048]{2,1,0:T(8,128)(2,1)S(1)}, bf16[16,16,2048]{2,1,0:T(8,128)(2,1)}, u32[]{:S(2)}) copy-start(bf16[16,16,2048]{2,1,0:T(8,128)(2,1)} %copy-done.2) | copy-start | bytes 3145732

commit v4 on v3

--- a/solution.py
+++ b/solution.py
@@ -282,7 +282,7 @@
         + [dma((2 * fars + 1,))] * 2
         + [dma((2 * fars,))] * 2,
         compiler_params=pltpu.CompilerParams(
-            collective_id=0, has_side_effects=True, vmem_limit_bytes=40 * 1024 * 1024
+            collective_id=0, has_side_effects=True, vmem_limit_bytes=54 * 1024 * 1024
         ),
     )(cot, send, weight)
 

time: 78.8 us -> 79.8 us (1.013)
  local copies, waits for them, and re-layouts: 7.24 us -> 2.43 us
  matrix products: 5.67 us -> 8.74 us
  Pallas kernels: 62.3 us -> 65 us
    unnamed x11 -> x9, local copies, waits for them, and re-layouts: 6.92 us -> 2.1 us
    pallas_call x1, Pallas kernels: 62.3 us -> 65 us  [layer(): pl.pallas_call(functools.partial(layer_kernel, n), out_shape=(jax.ShapeDt...]
    dot_general x1, matrix products: 1.04 us -> 2.34 us  [on_device(): lax.dot_general(cot_keep, hidden_rows, contract, preferred_element_type=j...]
    dot_general x1, matrix products: 0.46 us -> 1.46 us  [on_device(): lax.dot_general(placement, grad_back, (((0,), (0,)), ((), ())), preferred...]
where the time goes in v4:
time: 79.8 us; the launch traced here: 79.5 us
  Pallas kernels  65 us (81%)
  matrix products  8.74 us (11%)
  other arithmetic  2.54 us (3%)
  local copies, waits for them, and re-layouts  2.43 us (3%)
    pallas_call x1, Pallas kernels, layer(): pl.pallas_call(functools.partial(layer_kernel, n), out_shape=(jax.ShapeDt...  65 us
    dot_general x1, matrix products, on_device(): lax.dot_general(cot_other, hidden_other, contract, preferred_element_type...  3.83 us
    dot_general x1, matrix products, on_device(): lax.dot_general(cot_keep, hidden_rows, contract, preferred_element_type=j...  2.34 us
    unnamed x9, local copies, waits for them, and re-layouts  2.1 us

profile of v4, /device:TPU:0, one launch (start us, length us, event | category | flops | bytes accessed | tf_op | source)
XLA Modules:
  0.0 79.5 jit_solution(10785156153204996363)
XLA Ops:
  0.6 0.7 broadcast_multiply_fusion
  1.3 0.1 copy.12
  1.4 0.1 mul.58
  1.5 0.8 copy.13
  2.3 0.1 mul.59
  2.4 1.1 %bitcast_convert_fusion = f32[128,1536]{1,0:T(8,128)S(1)} fusion(bf16[16,8,1536]{2,1,0:T(8,128)(2,1)} %param.5), kind=kLoop, calls=%fused_computation.6 | loop fusion | flops 196608 | bytes 1179648 | tf_op jit(solution)/shard_map/convert_element_type | solution.py:303
  3.4 1.1 %convolution_convert_fusion = bf16[256,768]{1,0:T(8,128)(2,1)} fusion(f32[128]{0:T(128)S(1)} %mul.59, f32[128,1536]{1,0:T(8,128)S(1)} %bitcast_convert_fusion, s32[128]{0:T(128)S(1)} %fusion.10), kind=kOutput, calls=%fused_computation.2 | convolution fusion | flops 51249152 | bytes 1180672 | tf_op jit(solution)/shard_map/dot_general | solution.py:313
  4.5 65.0 %shard_map.84 = (bf16[16,16,4096]{2,1,0:T(8,128)(2,1)}, bf16[16,16,768]{2,1,0:T(8,128)(2,1)}, bf16[16,4096]{1,0:T(8,128)(2,1)}, bf16[16,16,768]{2,1,0:T(8,128)(2...) custom-call(bf16[16,4096]{1,0:T(8,128)(2,1)} %cot_ref.1, bf16[16,16,768]{2,1,0:T(8,128)(2,1)} %bitcast.25, ...), custom_call_target="tpu_custom_call" | custom-call | tf_op jit(solution)/shard_map/pallas_call | solution.py:252
  69.6 1.5 %fusion.6 = (bf16[16,8,768]{2,1,0:T(8,128)(2,1)S(1)}, bf16[16,8,768]{2,1,0:T(8,128)(2,1)S(1)}, f32[128]{0:T(128)S(1)}) fusion(f32[128,1536]{1,0:T(8,128)S(1)} %bitcast_convert_fusion, f32[128]{0:T(128)S(1)} %mul.59, bf16[256,768]{1,0:T(8,128)(2,1)} %bitcast.26, s32[128]{0:T(128)S(1)} %fusion.10), kind=kOutput, calls=%fused_computation.16 | convolution fusion | flops 52035456 | bytes 1574400 | tf_op jit(solution)/shard_map/dot_general | solution.py:360
  71.0 0.0 copy-start.1
  71.1 0.0 copy-start.2
  71.1 0.8 pad_maximum_fusion
  71.8 0.1 reshape.59
  71.9 0.7 copy.14
  72.6 2.3 %fusion.1 = f32[2048,768]{1,0:T(8,128)S(1)} fusion(bf16[256,768]{1,0:T(8,128)(2,1)} %bitcast.24, bf16[256,4096]{1,0:T(8,128)(2,1)} %bitcast.23, s32[]{:T(128)S(6)} %select_n.13), kind=kOutput, calls=%fused_computation.3 | convolution fusion | flops 805306368 | bytes 7733252 | tf_op jit(solution)/shard_map/dot_general | solution.py:345
  74.9 0.0 copy-done.1
  75.0 0.0 copy-done.2
  75.0 0.0 copy-start
  75.0 3.8 %fusion = f32[1,2048,768]{2,1,0:T(8,128)} fusion(f32[2048,768]{1,0:T(8,128)S(1)} %fusion.1, bf16[16,16,2048]{2,1,0:T(8,128)(2,1)S(1)} %copy-done.1, bf16[16,16,768]{2,1,0:T(8,128)(2,1)S(1)} %copy-done.2), kind=kOutput, calls=%fused_computation.1 | convolution fusion | flops 806879232 | bytes 14024704 | tf_op jit(solution)/shard_map/dot_general | solution.py:347
  78.8 0.0 copy-done
  78.8 0.7 copy.16
  (1 shorter events, 0.0 us)
Async XLA Ops:
  71.0 3.9 %copy-start.1 = (bf16[16,16,2048]{2,1,0:T(8,128)(2,1)S(1)}, bf16[16,16,2048]{2,1,0:T(8,128)(2,1)}, u32[]{:S(2)}) copy-start(bf16[16,16,2048]{2,1,0:T(8,128)(2,1)} %get-tuple-element.14) | copy-start | bytes 3145732
  71.1 3.9 %copy-start.2 = (bf16[16,16,768]{2,1,0:T(8,128)(2,1)S(1)}, bf16[16,16,768]{2,1,0:T(8,128)(2,1)}, u32[]{:S(2)}) copy-start(bf16[16,16,768]{2,1,0:T(8,128)(2,1)} %get-tuple-element.15) | copy-start | bytes 1179652
  75.0 3.8 %copy-start = (bf16[16,4096]{1,0:T(8,128)(2,1)S(1)}, bf16[16,4096]{1,0:T(8,128)(2,1)}, u32[]{:S(2)}) copy-start(bf16[16,4096]{1,0:T(8,128)(2,1)} %get-tuple-element.31) | copy-start | bytes 393220

commit v5 on v3

--- a/solution.py
+++ b/solution.py
@@ -116,17 +116,6 @@
     ]
     near_copies = [remote(cot_ref, cot_all.at[me], near_s.at[0], near_r.at[0], beside)]
     core_copies = [remote(cot_ref, cot_all.at[me], core_s.at[0], core_r.at[0], sibling)]
-    blocks = [me]
-    pairs = [pair(cot_ref.at[:, columns_there], cot_far.at[me], 0)]
-    for step in range(1, fars):
-        far_copies[step - 1].wait_recv()
-        block = ((far - step + fars) % fars) * 4 + near * 2 + core
-        ref = cot_all.at[block]
-        near_copies.append(remote(ref, ref, near_s.at[step], near_r.at[step], beside))
-        core_copies.append(remote(ref, ref, core_s.at[step], core_r.at[step], sibling))
-        pairs.append(pair(ref.at[:, columns_there], cot_far.at[block], step))
-        blocks.append(block)
-
     for copy in swap_copies:
         copy.wait_recv()
     keep_row.wait()
@@ -152,13 +141,15 @@
             )
         )
 
-    for step in range(fars):
-        near_copies[step].wait_recv()
-        block = ((far - step + fars) % fars) * 4 + (1 - near) * 2 + core
+    blocks = [me]
+    pairs = [pair(cot_ref.at[:, columns_there], cot_far.at[me], 0)]
+    for step in range(1, fars):
+        far_copies[step - 1].wait_recv()
+        block = ((far - step + fars) % fars) * 4 + near * 2 + core
         ref = cot_all.at[block]
-        at = fars + step
-        core_copies.append(remote(ref, ref, core_s.at[at], core_r.at[at], sibling))
-        pairs.append(pair(ref.at[:, columns_there], cot_far.at[block], at))
+        near_copies.append(remote(ref, ref, near_s.at[step], near_r.at[step], beside))
+        core_copies.append(remote(ref, ref, core_s.at[step], core_r.at[step], sibling))
+        pairs.append(pair(ref.at[:, columns_there], cot_far.at[block], step))
         blocks.append(block)
 
     onear = []
@@ -175,37 +166,18 @@
             )
         )
 
-    for copy in core_copies:
-        copy.wait_recv()
-    keep_cot.wait()
-    tile = hidden_units // 3 if hidden_units % 384 == 0 else hidden_units
-
-    @pl.loop(0, hidden_units // tile)
-    def _(at):
-        columns = pl.ds(pl.multiple_of(at * tile, tile), tile)
-        found = jnp.dot(
-            cot_all[...].reshape(n * tokens, width),
-            held[:, columns],
-            preferred_element_type=jnp.float32,
-        )
-        grad[:, :, columns] = found.astype(jnp.bfloat16).reshape(n, tokens, tile)
-
-    keep_grad = pltpu.make_async_copy(grad.at[me], back_ref.at[me], own_sem.at[3])
-    keep_grad.start()
-    oswap = []
-    for step in range(1, n):
-        target = (me + step) % n
-        oswap.append(
-            remote(
-                grad.at[target],
-                back_ref.at[me],
-                oswap_s.at[step - 1],
-                oswap_r.at[step - 1],
-                target,
-            )
-        )
+    for step in range(fars):
+        near_copies[step].wait_recv()
+        block = ((far - step + fars) % fars) * 4 + (1 - near) * 2 + core
+        ref = cot_all.at[block]
+        at = fars + step
+        core_copies.append(remote(ref, ref, core_s.at[at], core_r.at[at], sibling))
+        pairs.append(pair(ref.at[:, columns_there], cot_far.at[block], at))
+        blocks.append(block)
+
     ofar = []
-    for at in range(CHUNKS):
+
+    def push(at):
         onear[at].wait_recv()
         near_sum[at] = added(core_sum[at, :, near], near_buf[at])
         for step in range(1, fars):
@@ -220,6 +192,45 @@
                     target * 4 + near * 2 + core,
                 )
             )
+
+    for at in range(CHUNKS // 2):
+        push(at)
+    for copy in core_copies:
+        copy.wait_recv()
+    keep_cot.wait()
+    tile = hidden_units // 3 if hidden_units % 384 == 0 else hidden_units
+
+    @pl.loop(0, hidden_units // tile)
+    def _(at):
+        columns = pl.ds(pl.multiple_of(at * tile, tile), tile)
+        found = jnp.dot(
+            cot_all[...].reshape(n * tokens, width),
+            held[:, columns],
+            preferred_element_type=jnp.float32,
+        )
+        grad[:, :, columns] = found.astype(jnp.bfloat16).reshape(n, tokens, tile)
+
+    keep_grad = pltpu.make_async_copy(grad.at[me], back_ref.at[me], own_sem.at[3])
+    keep_grad.start()
+    oswap = []
+    for step in range(1, n):
+        target = (me + step) % n
+        oswap.append(
+            remote(
+                grad.at[target],
+                back_ref.at[me],
+                oswap_s.at[step - 1],
+                oswap_r.at[step - 1],
+                target,
+            )
+        )
+    for at in range(CHUNKS // 2, CHUNKS):
+        push(at)
+    passes = []
+    for at in range(2 * fars):
+        pairs[at].wait_recv()
+        ref = cot_far.at[blocks[at]]
+        passes.append(remote(ref, ref, pass_s.at[at], pass_r.at[at], sibling))
     for at in range(CHUNKS):
         for step in range(1, fars):
             ofar[at * (fars - 1) + step - 1].wait_recv()
@@ -227,11 +238,6 @@
         for step in range(1, fars):
             total = total + far_buf[at, step - 1].astype(jnp.float32)
         mixed_ref[:, at * chunk : (at + 1) * chunk] = total.astype(jnp.bfloat16)
-    passes = []
-    for at in range(2 * fars):
-        pairs[at].wait_recv()
-        ref = cot_far.at[blocks[at]]
-        passes.append(remote(ref, ref, pass_s.at[at], pass_r.at[at], sibling))
     for copy in oswap + passes + [row_pair]:
         copy.wait_recv()
     for copy in far_copies + near_copies + core_copies + swap_copies:

time: 78.8 us -> 77.4 us (0.982)
  Pallas kernels: 62.3 us -> 60.9 us
    pallas_call x1, Pallas kernels: 62.3 us -> 60.9 us  [layer(): pl.pallas_call(functools.partial(layer_kernel, n), out_shape=(jax.ShapeDt...]
where the time goes in v5:
time: 77.4 us; the launch traced here: 77.1 us
  Pallas kernels  60.9 us (79%)
  local copies, waits for them, and re-layouts  7.24 us (9%)
  matrix products  5.67 us (7%)
  other arithmetic  2.54 us (3%)
    pallas_call x1, Pallas kernels, layer(): pl.pallas_call(functools.partial(layer_kernel, n), out_shape=(jax.ShapeDt...  60.9 us
    unnamed x11, local copies, waits for them, and re-layouts  6.92 us
    dot_general x1, matrix products, on_device(): lax.dot_general(cot_other, hidden_other, contract, preferred_element_type...  3.82 us

profile of v5, /device:TPU:0, one launch (start us, length us, event | category | flops | bytes accessed | tf_op | source)
XLA Modules:
  0.0 77.1 jit_solution(12412168200413519165)
XLA Ops:
  0.6 0.7 broadcast_multiply_fusion
  1.3 0.1 copy.12
  1.4 0.1 mul.58
  1.5 0.8 copy.13
  2.3 0.1 mul.59
  2.4 1.1 %bitcast_convert_fusion = f32[128,1536]{1,0:T(8,128)S(1)} fusion(bf16[16,8,1536]{2,1,0:T(8,128)(2,1)} %param.5), kind=kLoop, calls=%fused_computation.6 | loop fusion | flops 196608 | bytes 1179648 | tf_op jit(solution)/shard_map/convert_element_type | solution.py:309
  3.4 0.4 convolution_convert_fusion
  3.8 0.0 copy-start
  3.8 2.8 %copy-done = bf16[1,4096,768]{2,1,0:T(8,128)(2,1)S(1)} copy-done((bf16[1,4096,768]{2,1,0:T(8,128)(2,1)S(1)}, bf16[1,4096,768]{2,1,0:T(8,128)(2,1)}, u32[]{:S(2)}) %copy-start) | copy-done | bytes 6291480
  6.6 0.0 copy-start.1
  6.6 0.9 %copy-done.1 = bf16[16,4096]{1,0:T(8,128)(2,1)S(1)} copy-done((bf16[16,4096]{1,0:T(8,128)(2,1)S(1)}, bf16[16,4096]{1,0:T(8,128)(2,1)}, u32[]{:S(2)}) %copy-start.1) | copy-done | bytes 131096
  7.5 60.9 %shard_map.84 = (bf16[16,16,4096]{2,1,0:T(8,128)(2,1)S(1)}, bf16[16,16,768]{2,1,0:T(8,128)(2,1)S(1)}, bf16[16,4096]{1,0:T(8,128)(2,1)S(1)}, bf16[16,16,768]{2,1,...) custom-call(bf16[16,4096]{1,0:T(8,128)(2,1)S(1)} %copy-done.1, ...), custom_call_target="tpu_custom_call" | custom-call | tf_op jit(solution)/shard_map/pallas_call | solution.py:258
  68.4 0.0 copy-start.2
  68.4 1.0 %copy-done.2 = bf16[16,16,2048]{2,1,0:T(8,128)(2,1)} copy-done((bf16[16,16,2048]{2,1,0:T(8,128)(2,1)}, bf16[16,16,2048]{2,1,0:T(8,128)(2,1)S(1)}, u32[]{:S(2)}) %copy-start.2) | copy-done | bytes 1048600
  69.4 0.5 fusion.6
  69.8 0.8 %pad_maximum_fusion = bf16[16,8,1536]{2,1,0:T(8,128)(2,1)} fusion(bf16[16,8,768]{2,1,0:T(8,128)(2,1)S(1)} %get-tuple-element.25, bf16[16,8,768]{2,1,0:T(8,128)(2,1)S(1)} %get-tuple-element.24), kind=kLoop, calls=%fused_computation.5 | loop fusion | flops 786432 | bytes 786432 | tf_op jit(solution)/shard_map/concatenate | solution.py:374
  70.6 0.1 reshape.59
  70.7 0.7 copy.14
  71.4 0.0 copy-start.3
  71.4 1.0 %fusion.1 = f32[2048,768]{1,0:T(8,128)S(1)} fusion(bf16[256,768]{1,0:T(8,128)(2,1)S(1)} %bitcast.24, bf16[256,4096]{1,0:T(8,128)(2,1)S(1)} %bitcast.23, s32[]{:T(128)S(6)} %select_n.13), kind=kOutput, calls=%fused_computation.3 | convolution fusion | flops 805306368 | bytes 7733252 | tf_op jit(solution)/shard_map/dot_general | solution.py:351
  72.4 0.2 copy-done.3
  72.6 3.8 %fusion = f32[1,2048,768]{2,1,0:T(8,128)} fusion(f32[2048,768]{1,0:T(8,128)S(1)} %fusion.1, bf16[16,16,2048]{2,1,0:T(8,128)(2,1)S(1)} %copy-done.3, bf16[16,16,768]{2,1,0:T(8,128)(2,1)S(1)} %get-tuple-element.15), kind=kOutput, calls=%fused_computation.1 | convolution fusion | flops 806879232 | bytes 14024704 | tf_op jit(solution)/shard_map/dot_general | solution.py:353
  76.4 0.7 copy.16
  (1 shorter events, 0.0 us)
Async XLA Ops:
  3.8 2.8 %copy-start = (bf16[1,4096,768]{2,1,0:T(8,128)(2,1)S(1)}, bf16[1,4096,768]{2,1,0:T(8,128)(2,1)}, u32[]{:S(2)}) copy-start(bf16[1,4096,768]{2,1,0:T(8,128)(2,1)} %param.8) | copy-start | bytes 18874372
  6.6 0.9 %copy-start.1 = (bf16[16,4096]{1,0:T(8,128)(2,1)S(1)}, bf16[16,4096]{1,0:T(8,128)(2,1)}, u32[]{:S(2)}) copy-start(bf16[16,4096]{1,0:T(8,128)(2,1)} %cot_ref.1) | copy-start | bytes 393220
  68.4 1.0 %copy-start.2 = (bf16[16,16,2048]{2,1,0:T(8,128)(2,1)}, bf16[16,16,2048]{2,1,0:T(8,128)(2,1)S(1)}, u32[]{:S(2)}) copy-start(bf16[16,16,2048]{2,1,0:T(8,128)(2,1)S(1)} %get-tuple-element.14) | copy-start | bytes 3145732
  71.4 1.2 %copy-start.3 = (bf16[16,16,2048]{2,1,0:T(8,128)(2,1)S(1)}, bf16[16,16,2048]{2,1,0:T(8,128)(2,1)}, u32[]{:S(2)}) copy-start(bf16[16,16,2048]{2,1,0:T(8,128)(2,1)} %copy-done.2) | copy-start | bytes 3145732
